TPU v7x, 256 devices: a whole 4x4x8 slice. The times are simulated.
256 devices in a mesh: src: 8 (over y, core), tgt: 32 (over x, z).
Axes of the slice: x: 4, y: 4, z: 8, core: 2. Of those that a mesh axis runs over, the one named last changes fastest.
Arguments:
- coupling: bfloat16 [8192, 32768], P('src', 'tgt'), may hold values from 0.099609375 to 1
- cost_src: bfloat16 [8192, 1536], P('src'), may hold values from -0.15625 to 0.15625
- cost_tgt: bfloat16 [32768, 1536], P('tgt'), may hold values from -0.15625 to 0.15625
- pattern: int32 [32, 128], P('src', 'tgt'), may hold values from 0 to 1, as said below
- mass_src: float32 [8192], P('src'), may hold values from 0.5 to 2
- mass_tgt: float32 [32768], P('tgt'), may hold values from 0.5 to 2
Outputs:
- new_coupling: float32 [8192, 32768], P('src', 'tgt')
Inputs may be any that keep to these rules, and one draw needn't show every extreme that they name: `pattern`: every row of tiles and every column of tiles holds at least one live tile.
All inputs are finite; a program needn't handle non-finite values.
Results may differ from a plain program's by a relative error of at most 0.0003.
Values may be sent and summed in bfloat16 or wider, within the bound.
No kernel may reach another device: no remote copies, remote signals or barrier semaphores. Data moves between devices by JAX's collectives and lax.ppermute only.
A program may use at most 64 MiB of HBM per device.

v0:
```python
import jax
import jax.numpy as jnp
from jax import lax
from jax.sharding import PartitionSpec as P

TILE = 256
H1 = 256
H2 = 256


step_size = 1.0


def with_halo(x, sides, width):
    for axis, dim in sides:
        size, length = (lax.axis_size(axis), x.shape[dim])
        up = [(i, (i + 1) % size) for i in range(size - 1)]
        down = [(j, i) for i, j in up]
        last = lax.slice_in_dim(x, length - width, length, axis=dim)
        initial = lax.slice_in_dim(x, 0, width, axis=dim)
        before = lax.ppermute(last, axis, up)
        after = lax.ppermute(initial, axis, down)
        x = jnp.concatenate([before, x, after], axis=dim)
    return x


def per_device(coupling, cost_src, cost_tgt, pattern, mass_src, mass_tgt):
    row_count, col_count = coupling.shape
    gate_tiles = pattern.astype(jnp.bfloat16)[:, None, :, None]
    masked = (
        coupling.reshape(pattern.shape[0], TILE, pattern.shape[1], TILE) * gate_tiles
    ).reshape(row_count, col_count)
    row_slab = with_halo(masked, (("src", 0),), H1)
    left_product = jnp.dot(cost_src, row_slab, preferred_element_type=jnp.float32)
    wide_product = with_halo(left_product, (("tgt", 1),), H2)
    grad_field = lax.dot_general(
        wide_product,
        cost_tgt.astype(jnp.float32),
        (((1,), (1,)), ((), ())),
        precision=lax.Precision.HIGHEST,
        preferred_element_type=jnp.float32,
    )
    kernel = masked.astype(jnp.float32) * jnp.exp(step_size * grad_field)
    row_total = lax.psum(jnp.sum(kernel, axis=1), "tgt")
    scaled = kernel * (mass_src * (col_count * lax.axis_size("tgt")) / row_total)[:, None]
    col_total = lax.psum(jnp.sum(scaled, axis=0), "src")
    return scaled * (mass_tgt * (row_count * lax.axis_size("src")) / col_total)[None, :]


def solution(mesh):
    return jax.shard_map(
        per_device,
        mesh=mesh,
        in_specs=(
            P("src", "tgt"),
            P("src", None),
            P("tgt", None),
            P("src", "tgt"),
            P("src"),
            P("tgt"),
        ),
        out_specs=P("src", "tgt"),
        check_vma=False,
    )
```

profile of v0, /device:TPU:1, one launch (start us, length us, event | category | flops | bytes accessed | tf_op | source)
XLA Modules:
  0.0 169.7 jit_solution(8548064655098570445)
XLA Ops:
  0.0 0.8 convert_element_type.7
  0.8 4.6 %reshape.10 = bf16[4,256,4,256]{3,2,1,0:T(4,128)(2,1)} reshape(bf16[1024,1024]{1,0:T(8,128)(2,1)} %param.6) | data formatting | bytes 4194304 | tf_op jit(solution)/shard_map/reshape | solution.py:31
  5.5 2.5 %broadcast_multiply_fusion = bf16[4,256,4,256]{3,2,1,0:T(4,128)(2,1)S(1)} fusion(bf16[4,256,4,256]{3,2,1,0:T(4,128)(2,1)} %reshape.10, bf16[4,4]{1,0:T(4,128)(2,1)S(1)} %convert_element_type.7), kind=kLoop, calls=%fused_computation.16 | loop fusion | flops 1048576 | bytes 4194336 | tf_op jit(solution)/shard_map/mul | solution.py:31
  8.0 0.4 fusion.20
  8.4 0.1 copy.9
  8.5 5.3 %collective-permute-start.1 = (bf16[256,1024]{1,0:T(8,128)(2,1)S(1)}, bf16[256,1024]{1,0:T(8,128)(2,1)S(1)}, u32[]{:S(2)}, u32[]{:S(2)}) collective-permute-start(bf16[256,1024]{1,0:T(8,128)(2,1)S(1)} %bitcast.17), channel_id=1, source_target_pairs={{32,0},{64,32},{96,64},{128,96},{160,128},{192,160},{224,192},{33,... | collective-permute-start | bytes 1572872 | tf_op jit(solution)/shard_map/ppermute | solution.py:22
  13.8 0.1 copy.8
  13.9 1.9 %collective-permute-start = (bf16[256,1024]{1,0:T(8,128)(2,1)S(1)}, bf16[256,1024]{1,0:T(8,128)(2,1)S(1)}, u32[]{:S(2)}, u32[]{:S(2)}) collective-permute-start(bf16[256,1024]{1,0:T(8,128)(2,1)S(1)} %bitcast.18), channel_id=1, source_target_pairs={{0,32},{32,64},{64,96},{96,128},{128,160},{160,192},{192,224},{1,3... | collective-permute-start | bytes 1572872 | tf_op jit(solution)/shard_map/ppermute | solution.py:21
  15.8 0.6 mul.44
  16.4 0.5 copy.7
  16.9 1.0 mul.46
  17.9 2.1 %collective-permute-done.1 = bf16[256,1024]{1,0:T(8,128)(2,1)S(1)} collective-permute-done((bf16[256,1024]{1,0:T(8,128)(2,1)S(1)}, bf16[256,1024]{1,0:T(8,128)(2,1)S(1)}, u32[]{:S(2)}, u32[]{:S(2)}) %collective-permute-start.1) | collective-permute-done | bytes 524320 | tf_op jit(solution)/shard_map/ppermute | solution.py:22
  20.1 1.8 %collective-permute-done = bf16[256,1024]{1,0:T(8,128)(2,1)S(1)} collective-permute-done((bf16[256,1024]{1,0:T(8,128)(2,1)S(1)}, bf16[256,1024]{1,0:T(8,128)(2,1)S(1)}, u32[]{:S(2)}, u32[]{:S(2)}) %collective-permute-start) | collective-permute-done | bytes 524320 | tf_op jit(solution)/shard_map/ppermute | solution.py:21
  21.9 3.5 %fusion.12 = f32[1024,1024]{0,1:T(8,128)S(1)} fusion(bf16[1024,1536]{1,0:T(8,128)(2,1)S(1)} %copy-done.4, bf16[256,1024]{1,0:T(8,128)(2,1)S(1)} %collective-permute-done.1, bf16[1024,1024]{1,0:T(8,128)(2,1)S(1)} %mul.46, bf16[256,1024]{1,0:T(8,128)(2,1)S(1)} %collective-permute-done), kind=kOutput, calls=%fused_computation.15 | convolution fusion | flops 3230662656 | bytes 10485760 | tf_op jit(solution)/shard_map/dot_general | solution.py:34
  25.4 0.2 fusion.19
  25.6 3.1 %collective-permute-start.2 = (f32[1024,256]{0,1:T(8,128)S(1)}, f32[1024,256]{0,1:T(8,128)S(1)}, u32[]{:S(2)}, u32[]{:S(2)}) collective-permute-start(f32[1024,256]{0,1:T(8,128)S(1)} %get-tuple-element.5), channel_id=1, source_target_pairs={{0,1},{1,2},{2,3},{3,4},{4,5},{5,6},{6,7},{7,8},{8,9},{9,10},{10,1... | collective-permute-start | bytes 3145736 | tf_op jit(solution)/shard_map/ppermute | solution.py:21
  28.7 1.5 collective-permute-start.3
  30.2 18.1 %collective-permute-done.2 = f32[1024,256]{0,1:T(8,128)S(1)} collective-permute-done((f32[1024,256]{0,1:T(8,128)S(1)}, f32[1024,256]{0,1:T(8,128)S(1)}, u32[]{:S(2)}, u32[]{:S(2)}) %collective-permute-start.2) | collective-permute-done | bytes 1048608 | tf_op jit(solution)/shard_map/ppermute | solution.py:21
  48.3 4.2 %collective-permute-done.3 = f32[1024,256]{0,1:T(8,128)S(1)} collective-permute-done((f32[1024,256]{0,1:T(8,128)S(1)}, f32[1024,256]{0,1:T(8,128)S(1)}, u32[]{:S(2)}, u32[]{:S(2)}) %collective-permute-start.3) | collective-permute-done | bytes 1048608 | tf_op jit(solution)/shard_map/ppermute | solution.py:22
  52.5 21.3 %fusion.21 = (f32[1024]{0:T(1024)S(1)}, f32[1024,1024]{1,0:T(8,128)}) fusion(bf16[1024,1536]{1,0:T(8,128)(2,1)S(1)} %copy-done, f32[1024,256]{0,1:T(8,128)S(1)} %collective-permute-done.3, f32[1024,1024]{0,1:T(8,128)S(1)} %fusion.12, f32[1024,256]{0,1:T(8,128)S(1)} %collective-permute-done.2, bf16[1024,1024]{1,0:T(8,128)(2,1)S(1)} %mul.46), kind=kOutput, calls=%fused_computation.23 | convolution fusion | flops 19333644288 | bytes 15732736 | tf_op jit(solution)/shard_map/dot_general | solution.py:36
  73.7 61.4 %psum.14 = f32[1024]{0:T(1024)S(1)} all-reduce(f32[1024]{0:T(1024)S(1)} %get-tuple-element.9), channel_id=1, replica_groups=mesh['src'=8,'tgt'=32] {'tgt'}, use_global_device_ids=true, to_apply=%region_1.0 | all-reduce | flops 1024 | bytes 8192 | tf_op jit(solution)/shard_map/psum | solution.py:44
  135.1 2.5 %multiply_reduce_fusion = f32[1024]{0:T(1024)S(1)} fusion(f32[1024,1024]{1,0:T(8,128)} %get-tuple-element.10, f32[1024]{0:T(1024)S(1)} %multiply_divide_fusion.1), kind=kLoop, calls=%fused_computation.8 | loop fusion | flops 2096128 | bytes 4202496 | tf_op jit(solution)/shard_map/reduce_sum | solution.py:46
  137.6 27.5 %psum.15 = f32[1024]{0:T(1024)S(1)} all-reduce(f32[1024]{0:T(1024)S(1)} %multiply_reduce_fusion), channel_id=1, replica_groups=mesh['src'=8,'tgt'=32] {'src'}, use_global_device_ids=true, to_apply=%region_3.0 | all-reduce | flops 1024 | bytes 8192 | tf_op jit(solution)/shard_map/psum | solution.py:46
  165.1 4.6 %multiply_multiply_fusion = f32[1024,1024]{1,0:T(8,128)} fusion(f32[1024,1024]{1,0:T(8,128)} %get-tuple-element.10, f32[1024]{0:T(1024)S(1)} %multiply_divide_fusion, f32[1024]{0:T(1024)S(1)} %multiply_divide_fusion.1), kind=kLoop, calls=%fused_computation.7 | loop fusion | flops 2097152 | bytes 8396800 | tf_op jit(solution)/shard_map/mul | solution.py:47
  (12 shorter events, 0.0 us)
Async XLA Ops:
  0.0 52.5 %copy-start = (bf16[1024,1536]{1,0:T(8,128)(2,1)S(1)}, bf16[1024,1536]{1,0:T(8,128)(2,1)}, u32[]{:S(2)}) copy-start(bf16[1024,1536]{1,0:T(8,128)(2,1)} %param.8) | copy-start | bytes 9437188
  8.4 8.6 %copy-start.1 = (bf16[1024,1024]{1,0:T(8,128)(2,1)S(1)}, bf16[1024,1024]{1,0:T(8,128)(2,1)}, u32[]{:S(2)}) copy-start(bf16[1024,1024]{1,0:T(8,128)(2,1)} %param.6) | copy-start | bytes 6291460
  8.5 11.6 %collective-permute-start.1 = (bf16[256,1024]{1,0:T(8,128)(2,1)S(1)}, bf16[256,1024]{1,0:T(8,128)(2,1)S(1)}, u32[]{:S(2)}, u32[]{:S(2)}) collective-permute-start(bf16[256,1024]{1,0:T(8,128)(2,1)S(1)} %bitcast.17), channel_id=1, source_target_pairs={{32,0},{64,32},{96,64},{128,96},{160,128},{192,160},{224,192},{33,... | collective-permute-start | bytes 1572872 | tf_op jit(solution)/shard_map/ppermute | solution.py:22
  13.9 8.0 %collective-permute-start = (bf16[256,1024]{1,0:T(8,128)(2,1)S(1)}, bf16[256,1024]{1,0:T(8,128)(2,1)S(1)}, u32[]{:S(2)}, u32[]{:S(2)}) collective-permute-start(bf16[256,1024]{1,0:T(8,128)(2,1)S(1)} %bitcast.18), channel_id=1, source_target_pairs={{0,32},{32,64},{64,96},{96,128},{128,160},{160,192},{192,224},{1,3... | collective-permute-start | bytes 1572872 | tf_op jit(solution)/shard_map/ppermute | solution.py:21
  16.9 5.0 %copy-start.4 = (bf16[1024,1536]{1,0:T(8,128)(2,1)S(1)}, bf16[1024,1536]{1,0:T(8,128)(2,1)}, u32[]{:S(2)}) copy-start(bf16[1024,1536]{1,0:T(8,128)(2,1)} %param.7) | copy-start | bytes 9437188
  25.6 22.7 %collective-permute-start.2 = (f32[1024,256]{0,1:T(8,128)S(1)}, f32[1024,256]{0,1:T(8,128)S(1)}, u32[]{:S(2)}, u32[]{:S(2)}) collective-permute-start(f32[1024,256]{0,1:T(8,128)S(1)} %get-tuple-element.5), channel_id=1, source_target_pairs={{0,1},{1,2},{2,3},{3,4},{4,5},{5,6},{6,7},{7,8},{8,9},{9,10},{10,1... | collective-permute-start | bytes 3145736 | tf_op jit(solution)/shard_map/ppermute | solution.py:21
  28.7 106.4 %copy-start.2 = (f32[1024]{0:T(1024)S(1)}, f32[1024]{0:T(1024)}, u32[]{:S(2)}) copy-start(f32[1024]{0:T(1024)} %param.10) | copy-start | bytes 12292
  28.7 23.8 %collective-permute-start.3 = (f32[1024,256]{0,1:T(8,128)S(1)}, f32[1024,256]{0,1:T(8,128)S(1)}, u32[]{:S(2)}, u32[]{:S(2)}) collective-permute-start(f32[1024,256]{0,1:T(8,128)S(1)} %get-tuple-element.6), channel_id=1, source_target_pairs={{1,0},{2,1},{3,2},{4,3},{5,4},{6,5},{7,6},{8,7},{9,8},{10,9},{11,1... | collective-permute-start | bytes 3145736 | tf_op jit(solution)/shard_map/ppermute | solution.py:22
  73.7 91.4 %copy-start.3 = (f32[1024]{0:T(1024)S(1)}, f32[1024]{0:T(1024)}, u32[]{:S(2)}) copy-start(f32[1024]{0:T(1024)} %param.11) | copy-start | bytes 12292
where the time goes:
time: 170 us
  blocking collectives  88.8 us (52%)
  waiting for transfers between devices  26.3 us (15%)
  matrix products  24.7 us (15%)
  starting transfers between devices  11.7 us (7%)
  other arithmetic  11.5 us (7%)
  local copies, waits for them, and re-layouts  6.53 us (4%)
    psum x1, blocking collectives, per_device(): row_total = lax.psum(jnp.sum(kernel, axis=1), 'tgt')  61.4 us
    psum x1, blocking collectives, per_device(): col_total = lax.psum(jnp.sum(scaled, axis=0), 'src')  27.5 us
    dot_general x1, matrix products, per_device(): lax.dot_general(wide_product, cost_tgt.astype(jnp.float32), (((1,), (1,))...  21.3 us
    ppermute x2, waiting for transfers between devices, with_halo(): before = lax.ppermute(last, axis, up)  19.9 us
    ppermute x2, starting transfers between devices, with_halo(): after = lax.ppermute(initial, axis, down)  6.75 us
    ppermute x2, waiting for transfers between devices, with_halo(): after = lax.ppermute(initial, axis, down)  6.32 us
    ppermute x2, starting transfers between devices, with_halo(): before = lax.ppermute(last, axis, up)  4.97 us
    reshape x1, local copies, waits for them, and re-layouts, per_device(): coupling.reshape(pattern.shape[0], TILE, pattern.shape[1], TILE)  4.61 us
  transfers between devices with their start and end apart: 4, of which 4 were waited for; matrix products, arithmetic and copies ran while one was open for 1% of the time, Pallas kernels for 0%

commit v1 on v0

v1 whole, which is shorter than its diff:
```python
import jax
import jax.numpy as jnp
from jax import lax
from jax.sharding import PartitionSpec as P

TILE = 256
H1 = 256
H2 = 256


step_size = 1.0


def pair_plans(size):
    near = [(i, i ^ 1) for i in range(size)]
    far = []
    for i in range(1, size - 1, 2):
        far += [(i, i + 1), (i + 1, i)]
    return near, far


def exchange(first, second, axis):
    near, far = pair_plans(lax.axis_size(axis))
    return lax.ppermute(first, axis, near), lax.ppermute(second, axis, far)


def total_over(x, axis):
    size = lax.axis_size(axis)
    copies = jnp.broadcast_to(x[None, :], (size, x.shape[0]))
    copies = lax.optimization_barrier(copies)
    return jnp.sum(lax.all_to_all(copies, axis, 0, 0), axis=0)


def split_dot(a, b):
    hi = lax.reduce_precision(a, 8, 7)
    lo = (a - hi).astype(jnp.bfloat16)
    dims = (((1,), (1,)), ((), ()))
    dot = lambda x: lax.dot_general(x, b, dims, preferred_element_type=jnp.float32)
    return dot(hi.astype(jnp.bfloat16)) + dot(lo)


def per_device(coupling, cost_src, cost_tgt, pattern, mass_src, mass_tgt):
    rows, cols = coupling.shape
    n_src, n_tgt = lax.axis_size("src"), lax.axis_size("tgt")
    odd_s = lax.axis_index("src") % 2
    odd_t = lax.axis_index("tgt") % 2

    row_tile = lax.broadcasted_iota(jnp.int32, (rows, cols), 0) // TILE
    col_tile = lax.broadcasted_iota(jnp.int32, (rows, cols), 1) // TILE
    gate = jnp.zeros((rows, cols), jnp.int32)
    for r in range(pattern.shape[0]):
        for c in range(pattern.shape[1]):
            gate = jnp.where((row_tile == r) & (col_tile == c), pattern[r, c], gate)
    masked = jnp.where(gate != 0, coupling, jnp.zeros_like(coupling))

    c_near = (1 - odd_t) * (cols - H2)
    c_far = odd_t * (cols - H2)
    r_near = (1 - odd_s) * (rows - H1)
    r_far = odd_s * (rows - H1)
    side = exchange(
        lax.dynamic_slice_in_dim(masked, c_near, H2, 1),
        lax.dynamic_slice_in_dim(masked, c_far, H2, 1),
        "tgt",
    )
    ends = exchange(
        lax.dynamic_slice_in_dim(masked, r_near, H1, 0),
        lax.dynamic_slice_in_dim(masked, r_far, H1, 0),
        "src",
    )
    sides = jnp.concatenate(side, axis=1)
    corners = exchange(
        lax.dynamic_slice_in_dim(sides, r_near, H1, 0),
        lax.dynamic_slice_in_dim(sides, r_far, H1, 0),
        "src",
    )

    s_own = cost_src[:, H1:H1 + rows]
    s_near = lax.dynamic_slice_in_dim(cost_src, (1 - odd_s) * (rows + H1), H1, 1)
    s_far = lax.dynamic_slice_in_dim(cost_src, odd_s * (rows + H1), H1, 1)
    t_own = cost_tgt[:, H2:H2 + cols]
    t_near = lax.dynamic_slice_in_dim(cost_tgt, (1 - odd_t) * (cols + H2), H2, 1)
    t_far = lax.dynamic_slice_in_dim(cost_tgt, odd_t * (cols + H2), H2, 1)
    s_ends = jnp.concatenate([s_near, s_far], axis=1)
    t_sides = jnp.concatenate([t_near, t_far], axis=1)

    dot = lambda a, b: jnp.dot(a, b, preferred_element_type=jnp.float32)
    left_own = dot(s_own, masked) + dot(s_ends, jnp.concatenate(ends, axis=0))
    grad = split_dot(left_own, t_own)
    left_sides = dot(s_own, sides) + dot(s_ends, jnp.concatenate(corners, axis=0))
    grad = grad + split_dot(left_sides, t_sides)

    kernel = masked.astype(jnp.float32) * jnp.exp(step_size * grad)
    row_total = total_over(jnp.sum(kernel, axis=1), "tgt")
    scaled = kernel * (mass_src * (cols * n_tgt) / row_total)[:, None]
    col_total = total_over(jnp.sum(scaled, axis=0), "src")
    return scaled * (mass_tgt * (rows * n_src) / col_total)[None, :]


def solution(mesh):
    return jax.shard_map(
        per_device,
        mesh=mesh,
        in_specs=(
            P("src", "tgt"),
            P("src", None),
            P("tgt", None),
            P("src", "tgt"),
            P("src"),
            P("tgt"),
        ),
        out_specs=P("src", "tgt"),
        check_vma=False,
    )
```

time: 170 us -> 100 us (0.59)
  blocking collectives: 88.8 us -> 31.4 us
  waiting for transfers between devices: 26.3 us -> 3.68 us
  other arithmetic: 11.5 us -> 26.1 us
  matrix products: 24.7 us -> 16.1 us
  local copies, waits for them, and re-layouts: 6.53 us -> 9.76 us
    psum x2 -> x0, blocking collectives: 88.8 us -> none  [the longest x1 61.4 us: per_device(): row_total = lax.psum(jnp.sum(kernel, axis=1), 'tgt')]
    all_to_all x0 -> x2, blocking collectives: none -> 31.4 us  [total_over(): return jnp.sum(lax.all_to_all(copies, axis, 0, 0), axis=0)]
    ppermute x4 -> x6, waiting for transfers between devices: 26.3 us -> 3.68 us  [exchange(): return (lax.ppermute(first, axis, near), lax.ppermute(second, axis, far))]
    select_n x0 -> x1, other arithmetic: none -> 18.8 us  [per_device(): masked = jnp.where(gate != 0, coupling, jnp.zeros_like(coupling))]
    dot_general x2 -> x8, matrix products: 24.7 us -> 16.1 us  [the longest x4 10.3 us: split_dot(): lax.dot_general(x, b, dims, preferred_element_type=jnp.float32)]
    dynamic_slice x0 -> x5, local copies, waits for them, and re-layouts: none -> 4.92 us  [the longest x1 1.43 us: per_device(): lax.dynamic_slice_in_dim(cost_src, (1 - odd_s) * (rows + H1), H1, 1)]
    reshape x1 -> x0, local copies, waits for them, and re-layouts: 4.61 us -> none  [per_device(): coupling.reshape(pattern.shape[0], TILE, pattern.shape[1], TILE)]
    mul x3 -> x1, other arithmetic: 8.14 us -> 4.61 us  [per_device(): return scaled * (mass_tgt * (rows * n_src) / col_total)[None, :]]
  transfers between devices with their start and end apart: 4 -> 6, of which waited for: 4 -> 3; matrix products, arithmetic and copies ran while one was open for 1% -> 15% of each run, Pallas kernels for 0% -> 0%
where the time goes in v1:
time: 100 us; the launch traced here: 99.5 us
  blocking collectives  31.4 us (31%)
  other arithmetic  26.1 us (26%)
  matrix products  16.1 us (16%)
  starting transfers between devices  12.1 us (12%)
  local copies, waits for them, and re-layouts  9.76 us (10%)
  waiting for transfers between devices  3.68 us (4%)
    all_to_all x2, blocking collectives, total_over(): return jnp.sum(lax.all_to_all(copies, axis, 0, 0), axis=0)  31.4 us
    select_n x1, other arithmetic, per_device(): masked = jnp.where(gate != 0, coupling, jnp.zeros_like(coupling))  18.8 us
    ppermute x6, starting transfers between devices, exchange(): return (lax.ppermute(first, axis, near), lax.ppermute(second, axis, far))  12.1 us
    dot_general x4, matrix products, split_dot(): lax.dot_general(x, b, dims, preferred_element_type=jnp.float32)  10.3 us
    dot_general x4, matrix products, per_device(): dot = lambda a, b: jnp.dot(a, b, preferred_element_type=jnp.float32)  5.79 us
    mul x1, other arithmetic, per_device(): return scaled * (mass_tgt * (rows * n_src) / col_total)[None, :]  4.61 us
    ppermute x6, waiting for transfers between devices, exchange(): return (lax.ppermute(first, axis, near), lax.ppermute(second, axis, far))  3.68 us
    reduce_sum x1, other arithmetic, per_device(): col_total = total_over(jnp.sum(scaled, axis=0), 'src')  2.53 us
  transfers between devices with their start and end apart: 6, of which 3 were waited for; matrix products, arithmetic and copies ran while one was open for 15% of the time, Pallas kernels for 0%

profile of v1, /device:TPU:1, one launch (start us, length us, event | category | flops | bytes accessed | tf_op | source)
XLA Modules:
  0.0 99.5 jit_solution(16488832614078739841)
XLA Ops:
  0.0 2.0 %fusion.44 = (s32[1,1]{1,0:T(1,128)}, s32[1,1]{1,0:T(1,128)}, s32[1,1]{1,0:T(1,128)}, s32[1,1]{1,0:T(1,128)}, s32[1,1]{1,0:T(1,128)}, /*index=5*/s32[1,1]{1,0:T(...) fusion(s32[4,4]{1,0:T(4,128)} %param.9), kind=kLoop, calls=%fused_computation.80 | loop fusion | bytes 128 | tf_op jit(solution)/shard_map/slice | solution.py:53
  2.0 18.8 %fusion.17 = bf16[1024,1024]{1,0:T(8,128)(2,1)S(1)} fusion(bf16[1024,1024]{1,0:T(8,128)(2,1)} %param.6, s32[]{:T(128)} %bitcast.15, s32[]{:T(128)} %bitcast.14, s32[]{:T(128)} %bitcast.13, s32[]{:T(128)} %bitcast.12, s32[]{:T(128)} %bitcast.11, s32[]{:T(128)} %bitcast.10, s32[]{:T(128)} %bitcast.9, s32[]{:T(128)} %bitcast.8, s32[]{:T(128)} %bitcast.7, ...), kind=kLoop, calls=%fused_computation.30 | loop fusion | flops 46137344 | bytes 4203584 | tf_op jit(solution)/shard_map/jit(_where)/select_n | solution.py:54
  21.9 3.2 %collective-permute-start = (bf16[256,1024]{1,0:T(8,128)(2,1)}, bf16[256,1024]{1,0:T(8,128)(2,1)S(1)}, u32[]{:S(2)}, u32[]{:S(2)}) collective-permute-start(bf16[256,1024]{1,0:T(8,128)(2,1)} %get-tuple-element.9), channel_id=1, source_target_pairs={{0,32},{32,0},{64,96},{96,64},{128,160},{160,128},{192,224},{224,1... | collective-permute-start | bytes 1572872 | tf_op jit(solution)/shard_map/ppermute | solution.py:24
  25.1 1.9 %collective-permute-start.1 = (bf16[256,1024]{1,0:T(8,128)(2,1)}, bf16[256,1024]{1,0:T(8,128)(2,1)S(1)}, u32[]{:S(2)}, u32[]{:S(2)}) collective-permute-start(bf16[256,1024]{1,0:T(8,128)(2,1)} %get-tuple-element.10), channel_id=1, source_target_pairs={{32,64},{64,32},{96,128},{128,96},{160,192},{192,160},{33,65},{65,... | collective-permute-start | bytes 1572872 | tf_op jit(solution)/shard_map/ppermute | solution.py:24
  27.0 1.1 %constant_dynamic-slice_fusion.4 = (bf16[1024,256]{1,0:T(8,128)(2,1)}, bf16[1024,256]{1,0:T(8,128)(2,1)}) fusion(bf16[1024,1024]{1,0:T(8,128)(2,1)S(1)} %fusion.17, s32[]{:T(128)S(6)} %select_n.184, s32[]{:T(128)S(6)} %select_n.183), kind=kLoop, calls=%fused_computation.69 | loop fusion | bytes 2097160 | tf_op jit(solution)/shard_map/dynamic_slice | solution.py:62
  28.1 1.1 %collective-permute-start.2 = (bf16[1024,256]{1,0:T(8,128)(2,1)}, bf16[1024,256]{1,0:T(8,128)(2,1)}, u32[]{:S(2)}, u32[]{:S(2)}) collective-permute-start(bf16[1024,256]{1,0:T(8,128)(2,1)} %get-tuple-element.12), channel_id=1, source_target_pairs={{0,1},{1,0},{2,3},{3,2},{4,5},{5,4},{6,7},{7,6},{8,9},{9,8},{10,11... | collective-permute-start | bytes 1572872 | tf_op jit(solution)/shard_map/ppermute | solution.py:24
  29.2 1.5 %collective-permute-start.3 = (bf16[1024,256]{1,0:T(8,128)(2,1)}, bf16[1024,256]{1,0:T(8,128)(2,1)}, u32[]{:S(2)}, u32[]{:S(2)}) collective-permute-start(bf16[1024,256]{1,0:T(8,128)(2,1)} %get-tuple-element.11), channel_id=1, source_target_pairs={{1,2},{2,1},{3,4},{4,3},{5,6},{6,5},{7,8},{8,7},{9,10},{10,9},{11,... | collective-permute-start | bytes 1572872 | tf_op jit(solution)/shard_map/ppermute | solution.py:24
  30.7 1.4 %constant_dynamic-slice_fusion.9 = (bf16[1024,256]{1,0:T(8,128)(2,1)S(1)}, bf16[1024,256]{1,0:T(8,128)(2,1)S(1)}) fusion(bf16[1024,1536]{1,0:T(8,128)(2,1)} %param.7, s32[]{:T(128)S(6)} %select_n.178, s32[]{:T(128)S(6)} %select_n.179), kind=kLoop, calls=%fused_computation.74 | loop fusion | bytes 2097160 | tf_op jit(solution)/shard_map/dynamic_slice | solution.py:78
  32.1 1.3 %constant_dynamic-slice_fusion.1 = (bf16[1024,256]{1,0:T(8,128)(2,1)S(1)}, bf16[1024,256]{1,0:T(8,128)(2,1)S(1)}) fusion(bf16[1024,1536]{1,0:T(8,128)(2,1)} %param.8, s32[]{:T(128)S(6)} %select_n.185, s32[]{:T(128)S(6)} %select_n.186), kind=kLoop, calls=%fused_computation.66 | loop fusion | bytes 2097160 | tf_op jit(solution)/shard_map/dynamic_slice | solution.py:81
  33.4 2.4 %fusion.26 = f32[1024,1024]{1,0:T(8,128)S(1)} fusion(bf16[1024,1024]{1,0:T(8,128)(2,1)S(1)} %fusion.17, bf16[1024,1536]{1,0:T(8,128)(2,1)S(1)} %copy-done.1), kind=kOutput, calls=%fused_computation.43 | convolution fusion | flops 2147483648 | bytes 8388608 | tf_op jit(solution)/shard_map/dot_general | solution.py:86
  36.2 1.3 %bitcast_add_fusion = f32[1024,1024]{0,1:T(8,128)S(1)} fusion(f32[1024,1024]{1,0:T(8,128)S(1)} %fusion.26, bf16[256,1024]{1,0:T(8,128)(2,1)S(1)} %collective-permute-done.1, bf16[256,1024]{1,0:T(8,128)(2,1)S(1)} %collective-permute-done, bf16[1024,256]{1,0:T(8,128)(2,1)S(1)} %get-tuple-element.8, bf16[1024,256]{1,0:T(8,128)(2,1)S(1)} %get-tuple-element.7), kind=kOutput, calls=%fused_computation.27 | convolution fusion | flops 1078984704 | bytes 10485760 | tf_op jit(solution)/shard_map/dot_general | solution.py:86
  38.1 2.4 %fusion.19 = f32[1024,1024]{1,0:T(8,128)S(1)} fusion(f32[1024,1024]{0,1:T(8,128)S(1)} %bitcast_add_fusion, bf16[1024,1536]{1,0:T(8,128)(2,1)S(1)} %copy-done), kind=kOutput, calls=%fused_computation.36 | convolution fusion | flops 2150629376 | bytes 10485760 | tf_op jit(solution)/shard_map/dot_general | solution.py:38
  41.4 1.1 %constant_dynamic-update-slice_fusion.1 = bf16[1024,512]{1,0:T(8,128)(2,1)S(1)} fusion(bf16[1024,256]{1,0:T(8,128)(2,1)} %collective-permute-done.2), kind=kLoop, calls=%fused_computation.59 | loop fusion | bytes 1048576
  42.4 2.4 %fusion.21 = f32[1024,1024]{1,0:T(8,128)S(1)} fusion(f32[1024,1024]{0,1:T(8,128)S(1)} %bitcast_add_fusion, bf16[1024,1536]{1,0:T(8,128)(2,1)S(1)} %copy-done), kind=kOutput, calls=%fused_computation.37 | convolution fusion | flops 2149580800 | bytes 10485760 | tf_op jit(solution)/shard_map/dot_general | solution.py:38
  44.9 1.1 %constant_dynamic-update-slice_fusion = bf16[1024,512]{1,0:T(8,128)(2,1)S(1)} fusion(bf16[1024,512]{1,0:T(8,128)(2,1)S(1)} %constant_dynamic-update-slice_fusion.1, bf16[1024,256]{1,0:T(8,128)(2,1)} %collective-permute-done.3), kind=kLoop, calls=%fused_computation.58 | loop fusion | bytes 1048576 | tf_op jit(solution)/shard_map/concatenate | solution.py:70
  46.1 4.4 %collective-permute-start.5 = (bf16[256,512]{1,0:T(8,128)(2,1)S(1)}, bf16[256,512]{1,0:T(8,128)(2,1)S(1)}, u32[]{:S(2)}, u32[]{:S(2)}) collective-permute-start(bf16[256,512]{1,0:T(8,128)(2,1)S(1)} %get-tuple-element.14), channel_id=1, source_target_pairs={{32,64},{64,32},{96,128},{128,96},{160,192},{192,160},{33,65},{65,... | collective-permute-start | bytes 786440 | tf_op jit(solution)/shard_map/ppermute | solution.py:24
  50.5 1.3 %fusion.24 = f32[512,1024]{1,0:T(8,128)S(1)} fusion(bf16[1024,512]{1,0:T(8,128)(2,1)S(1)} %constant_dynamic-update-slice_fusion, bf16[1024,1536]{1,0:T(8,128)(2,1)S(1)} %copy-done.1), kind=kOutput, calls=%fused_computation.41 | convolution fusion | flops 1073741824 | bytes 5242880 | tf_op jit(solution)/shard_map/dot_general | solution.py:86
  51.8 2.5 %collective-permute-done.5 = bf16[256,512]{1,0:T(8,128)(2,1)S(1)} collective-permute-done((bf16[256,512]{1,0:T(8,128)(2,1)S(1)}, bf16[256,512]{1,0:T(8,128)(2,1)S(1)}, u32[]{:S(2)}, u32[]{:S(2)}) %collective-permute-start.5) | collective-permute-done | bytes 262176 | tf_op jit(solution)/shard_map/ppermute | solution.py:24
  55.1 1.3 %fusion.29 = f32[1024,1024]{1,0:T(8,128)S(1)} fusion(f32[1024,512]{0,1:T(8,128)S(1)} %fusion.33, f32[512,1024]{1,0:T(8,128)S(1)} %fusion.24, bf16[1024,256]{1,0:T(8,128)(2,1)S(1)} %get-tuple-element.6, bf16[1024,256]{1,0:T(8,128)(2,1)S(1)} %get-tuple-element.5), kind=kOutput, calls=%fused_computation.45 | convolution fusion | flops 1077411840 | bytes 9437184 | tf_op jit(solution)/shard_map/dot_general | solution.py:38
  56.4 4.2 %fusion.45 = (f32[1024]{0:T(1024)S(1)}, f32[1024,1024]{1,0:T(8,128)}) fusion(f32[1024,1024]{1,0:T(8,128)S(1)} %fusion.29, bf16[1024,256]{1,0:T(8,128)(2,1)S(1)} %get-tuple-element.6, bf16[1024,256]{1,0:T(8,128)(2,1)S(1)} %get-tuple-element.5, f32[1024,512]{0,1:T(8,128)S(1)} %fusion.33, f32[512,1024]{1,0:T(8,128)S(1)} %fusion.24, ...), kind=kOutput, calls=%fused_computation.81 | convolution fusion | flops 1084226560 | bytes 24121344 | tf_op jit(solution)/shard_map/dot_general | solution.py:38
  60.7 20.1 %all_to_all.18 = f32[32,1,1024]{2,1,0:T(1,128)S(1)} all-to-all(f32[32,1,1024]{2,1,0:T(1,128)S(1)} %all_to_all.12), channel_id=1, replica_groups=mesh['src'=8,'tgt'=32] {'tgt'}, dimensions={0} | all-to-all | bytes 262144 | tf_op jit(solution)/shard_map/all_to_all | solution.py:31
  80.9 2.5 %multiply_reduce_fusion = f32[1024]{0:T(1024)S(1)} fusion(f32[1024,1024]{1,0:T(8,128)} %get-tuple-element.32, f32[1024]{0:T(1024)S(1)} %multiply_divide_fusion.1), kind=kLoop, calls=%fused_computation.32 | loop fusion | flops 2096128 | bytes 4202496 | tf_op jit(solution)/shard_map/reduce_sum | solution.py:95
  83.5 11.3 %all_to_all.19 = f32[8,1,1024]{2,1,0:T(1,128)S(1)} all-to-all(f32[8,1,1024]{2,1,0:T(1,128)S(1)} %all_to_all.14), channel_id=1, replica_groups=mesh['src'=8,'tgt'=32] {'src'}, dimensions={0} | all-to-all | bytes 65536 | tf_op jit(solution)/shard_map/all_to_all | solution.py:31
  94.9 4.6 %multiply_multiply_fusion = f32[1024,1024]{1,0:T(8,128)} fusion(f32[1024,1024]{1,0:T(8,128)} %get-tuple-element.32, f32[1024]{0:T(1024)S(1)} %multiply_divide_fusion, f32[1024]{0:T(1024)S(1)} %multiply_divide_fusion.1), kind=kLoop, calls=%fused_computation.31 | loop fusion | flops 2097152 | bytes 8396800 | tf_op jit(solution)/shard_map/mul | solution.py:96
  (27 shorter events, 4.0 us)
Async XLA Ops:
  21.9 14.0 %collective-permute-start = (bf16[256,1024]{1,0:T(8,128)(2,1)}, bf16[256,1024]{1,0:T(8,128)(2,1)S(1)}, u32[]{:S(2)}, u32[]{:S(2)}) collective-permute-start(bf16[256,1024]{1,0:T(8,128)(2,1)} %get-tuple-element.9), channel_id=1, source_target_pairs={{0,32},{32,0},{64,96},{96,64},{128,160},{160,128},{192,224},{224,1... | collective-permute-start | bytes 1572872 | tf_op jit(solution)/shard_map/ppermute | solution.py:24
  25.1 11.1 %collective-permute-start.1 = (bf16[256,1024]{1,0:T(8,128)(2,1)}, bf16[256,1024]{1,0:T(8,128)(2,1)S(1)}, u32[]{:S(2)}, u32[]{:S(2)}) collective-permute-start(bf16[256,1024]{1,0:T(8,128)(2,1)} %get-tuple-element.10), channel_id=1, source_target_pairs={{32,64},{64,32},{96,128},{128,96},{160,192},{192,160},{33,65},{65,... | collective-permute-start | bytes 1572872 | tf_op jit(solution)/shard_map/ppermute | solution.py:24
  28.1 13.2 %collective-permute-start.2 = (bf16[1024,256]{1,0:T(8,128)(2,1)}, bf16[1024,256]{1,0:T(8,128)(2,1)}, u32[]{:S(2)}, u32[]{:S(2)}) collective-permute-start(bf16[1024,256]{1,0:T(8,128)(2,1)} %get-tuple-element.12), channel_id=1, source_target_pairs={{0,1},{1,0},{2,3},{3,2},{4,5},{5,4},{6,7},{7,6},{8,9},{9,8},{10,11... | collective-permute-start | bytes 1572872 | tf_op jit(solution)/shard_map/ppermute | solution.py:24
  29.2 15.6 %collective-permute-start.3 = (bf16[1024,256]{1,0:T(8,128)(2,1)}, bf16[1024,256]{1,0:T(8,128)(2,1)}, u32[]{:S(2)}, u32[]{:S(2)}) collective-permute-start(bf16[1024,256]{1,0:T(8,128)(2,1)} %get-tuple-element.11), channel_id=1, source_target_pairs={{1,2},{2,1},{3,4},{4,3},{5,6},{6,5},{7,8},{8,7},{9,10},{10,9},{11,... | collective-permute-start | bytes 1572872 | tf_op jit(solution)/shard_map/ppermute | solution.py:24
  30.7 2.7 %copy-start.1 = (bf16[1024,1536]{1,0:T(8,128)(2,1)S(1)}, bf16[1024,1536]{1,0:T(8,128)(2,1)}, u32[]{:S(2)}) copy-start(bf16[1024,1536]{1,0:T(8,128)(2,1)} %param.7) | copy-start | bytes 9437188
  36.2 1.9 %copy-start = (bf16[1024,1536]{1,0:T(8,128)(2,1)S(1)}, bf16[1024,1536]{1,0:T(8,128)(2,1)}, u32[]{:S(2)}) copy-start(bf16[1024,1536]{1,0:T(8,128)(2,1)} %param.8) | copy-start | bytes 9437188
  46.0 5.8 %collective-permute-start.4 = (bf16[256,512]{1,0:T(8,128)(2,1)S(1)}, bf16[256,512]{1,0:T(8,128)(2,1)S(1)}, u32[]{:S(2)}, u32[]{:S(2)}) collective-permute-start(bf16[256,512]{1,0:T(8,128)(2,1)S(1)} %get-tuple-element.13), channel_id=1, source_target_pairs={{0,32},{32,0},{64,96},{96,64},{128,160},{160,128},{192,224},{224,1... | collective-permute-start | bytes 786440 | tf_op jit(solution)/shard_map/ppermute | solution.py:24
  46.1 8.2 %collective-permute-start.5 = (bf16[256,512]{1,0:T(8,128)(2,1)S(1)}, bf16[256,512]{1,0:T(8,128)(2,1)S(1)}, u32[]{:S(2)}, u32[]{:S(2)}) collective-permute-start(bf16[256,512]{1,0:T(8,128)(2,1)S(1)} %get-tuple-element.14), channel_id=1, source_target_pairs={{32,64},{64,32},{96,128},{128,96},{160,192},{192,160},{33,65},{65,... | collective-permute-start | bytes 786440 | tf_op jit(solution)/shard_map/ppermute | solution.py:24
  56.4 24.5 %copy-start.2 = (f32[1024]{0:T(1024)S(1)}, f32[1024]{0:T(1024)}, u32[]{:S(2)}) copy-start(f32[1024]{0:T(1024)} %param.10) | copy-start | bytes 12292
  60.6 34.3 %copy-start.3 = (f32[1024]{0:T(1024)S(1)}, f32[1024]{0:T(1024)}, u32[]{:S(2)}) copy-start(f32[1024]{0:T(1024)} %param.11) | copy-start | bytes 12292

commit v2 on v0

v2 whole, which is shorter than its diff:
```python
import jax
import jax.numpy as jnp
from jax import lax
from jax.experimental import pallas as pl
from jax.experimental.pallas import tpu as pltpu
from jax.sharding import PartitionSpec as P

TILE = 256
H1 = 256
H2 = 256
LANES = 128

step_size = 1.0

f32 = jnp.float32
bf16 = jnp.bfloat16
VMEM = pltpu.VMEM
MIB = 1 << 20


def odd(axis):
    return lax.rem(lax.axis_index(axis), 2)


def at(parity, last):
    return pl.multiple_of(parity * last, TILE)


def dot(a, b):
    return jnp.dot(a, b, preferred_element_type=f32)


def dot_t(a, b):
    return lax.dot_general(a, b, (((1,), (1,)), ((), ())), preferred_element_type=f32)


def halves(x):
    hi = x.astype(bf16)
    return hi, (x - hi.astype(f32)).astype(bf16)


def as_row(x):
    return jnp.sum(x.T, axis=0, keepdims=True)


def mask_kernel(pattern, coupling, masked, c_near, c_far, r_near, r_far, raw, sems):
    rows, cols = masked.shape
    tiles_r, tiles_c = rows // TILE, cols // TILE

    def copy(r):
        part = pl.ds(r * TILE, TILE)
        return pltpu.make_async_copy(coupling.at[part], raw.at[part], sems.at[r])

    for r in range(tiles_r):
        copy(r).start()
    odd_s, odd_t = odd("src"), odd("tgt")
    c_last, r_last = cols - H2, rows - H1
    for r in range(tiles_r):
        copy(r).wait()
        part = slice(r * TILE, (r + 1) * TILE)
        for c in range(tiles_c):
            across = slice(c * TILE, (c + 1) * TILE)
            tile = raw[part, across]
            masked[part, across] = jnp.where(pattern[r, c] != 0, tile, jnp.zeros_like(tile))
        c_near[part, :] = masked[part, pl.ds(at(1 - odd_t, c_last), H2)]
        c_far[part, :] = masked[part, pl.ds(at(odd_t, c_last), H2)]
    r_near[...] = masked[pl.ds(at(1 - odd_s, r_last), H1), :]
    r_far[...] = masked[pl.ds(at(odd_s, r_last), H1), :]


def left_kernel(masked, r_near, r_far, cost_src, hi, lo):
    rows, cols = masked.shape
    odd_s = odd("src")
    s_near = pl.ds(at(1 - odd_s, rows + H1), H1)
    s_far = pl.ds(at(odd_s, rows + H1), H1)

    @pl.loop(0, cols // TILE)
    def _(n):
        across = pl.ds(pl.multiple_of(n * TILE, TILE), TILE)
        left = dot(cost_src[:, H1:H1 + rows], masked[:, across])
        left += dot(cost_src[:, s_near], r_near[:, across])
        left += dot(cost_src[:, s_far], r_far[:, across])
        hi[:, across], lo[:, across] = halves(left)


def own_kernel(hi, lo, cost_tgt, grad):
    rows, cols = grad.shape

    @pl.loop(0, cols // TILE)
    def _(n):
        across = pl.ds(pl.multiple_of(n * TILE, TILE), TILE)
        costs = cost_tgt[across, H2:H2 + cols]
        grad[:, across] = dot_t(hi[...], costs) + dot_t(lo[...], costs)


def tail_kernel(c_near, c_far, x_near, x_far, cost_src, cost_tgt, grad, masked,
                kernel, totals, hi, lo, part):
    rows, cols = masked.shape
    odd_s, odd_t = odd("src"), odd("tgt")
    s_near = pl.ds(at(1 - odd_s, rows + H1), H1)
    s_far = pl.ds(at(odd_s, rows + H1), H1)
    for n, side in ((0, c_near), (1, c_far)):
        across = slice(n * H2, (n + 1) * H2)
        left = dot(cost_src[:, H1:H1 + rows], side[...])
        left += dot(cost_src[:, s_near], x_near[:, across])
        left += dot(cost_src[:, s_far], x_far[:, across])
        hi[:, across], lo[:, across] = halves(left)
    part[...] = jnp.zeros_like(part)

    @pl.loop(0, cols // TILE)
    def _(n):
        across = pl.ds(pl.multiple_of(n * TILE, TILE), TILE)
        g = grad[:, across]
        for k, start in ((0, 1 - odd_t), (1, odd_t)):
            of = slice(k * H2, (k + 1) * H2)
            costs = cost_tgt[across, pl.ds(at(start, cols + H2), H2)]
            g += dot_t(hi[:, of], costs) + dot_t(lo[:, of], costs)
        value = masked[:, across].astype(f32) * jnp.exp(step_size * g)
        kernel[:, across] = value
        part[...] += value[:, :LANES] + value[:, LANES:]

    totals[...] = jnp.broadcast_to(as_row(part[...]), totals.shape)


def column_kernel(total, row_totals, mass, kernel, scaled, totals):
    rows, cols = kernel.shape
    factor = mass[...] * total / jnp.sum(row_totals[...], axis=0, keepdims=True)
    factor = jnp.broadcast_to(factor, (LANES, rows)).T
    for n in range(cols // LANES):
        across = slice(n * LANES, (n + 1) * LANES)
        value = kernel[:, across] * factor
        scaled[:, across] = value
        sums = jnp.sum(value, axis=0, keepdims=True)
        totals[:, across] = jnp.broadcast_to(sums, (totals.shape[0], LANES))


def last_kernel(total, col_totals, mass, scaled, out, block, sems):
    rows, cols = scaled.shape
    factor = mass[...] * total / jnp.sum(col_totals[...], axis=0, keepdims=True)
    n_blocks = sems.shape[0]
    size = rows // n_blocks

    def copy(n):
        part = pl.ds(n * size, size)
        return pltpu.make_async_copy(block.at[part], out.at[part], sems.at[n])

    for n in range(n_blocks):
        part = slice(n * size, (n + 1) * size)
        block[part, :] = scaled[part, :] * factor
        copy(n).start()
    for n in range(n_blocks):
        copy(n).wait()


def call(body, inputs, outputs, scratch, spaces=None, limit=16, flops=0, moved=0, exps=0):
    spaces = spaces or [VMEM] * len(inputs)
    args = [
        pltpu.with_memory_space_constraint(x, VMEM) if s is VMEM else x
        for x, s in zip(inputs, spaces)
    ]
    single = len(outputs) == 1
    shapes = [s if isinstance(s, jax.ShapeDtypeStruct) else VMEM(*s) for s in outputs]
    out_specs = [
        pl.BlockSpec(memory_space=pl.ANY if isinstance(s, jax.ShapeDtypeStruct) else VMEM)
        for s in outputs
    ]
    return pl.pallas_call(
        body,
        out_shape=shapes[0] if single else shapes,
        in_specs=[pl.BlockSpec(memory_space=s) for s in spaces],
        out_specs=out_specs[0] if single else out_specs,
        scratch_shapes=scratch,
        cost_estimate=pl.CostEstimate(flops=flops, bytes_accessed=moved, transcendentals=exps),
        compiler_params=pltpu.CompilerParams(vmem_limit_bytes=limit * MIB),
    )(*args)


def pair_plans(size):
    near = [(i, i ^ 1) for i in range(size)]
    far = []
    for i in range(1, size - 1, 2):
        far += [(i, i + 1), (i + 1, i)]
    return near, far


def exchange(first, second, axis):
    near, far = pair_plans(lax.axis_size(axis))
    return lax.ppermute(first, axis, near), lax.ppermute(second, axis, far)


def per_device(coupling, cost_src, cost_tgt, pattern, mass_src, mass_tgt):
    rows, cols = coupling.shape
    n_src, n_tgt = lax.axis_size("src"), lax.axis_size("tgt")
    tiles = pattern.shape[0]
    dma = pltpu.SemaphoreType.DMA

    masked, c_near, c_far, r_near, r_far = call(
        mask_kernel,
        [pattern, coupling],
        [((rows, cols), bf16)] + [((rows, H2), bf16)] * 2 + [((H1, cols), bf16)] * 2,
        [VMEM((rows, cols), bf16), dma((tiles,))],
        spaces=[pltpu.SMEM, pl.ANY],
        moved=6 * MIB,
    )
    c_near, c_far = exchange(c_near, c_far, "tgt")
    r_near, r_far = exchange(r_near, r_far, "src")
    hi, lo = call(
        left_kernel,
        [masked, r_near, r_far, cost_src],
        [((rows, cols), bf16)] * 2,
        [],
        flops=2 * rows * cols * (cols + 2 * H1),
        moved=10 * MIB,
    )
    c_near, c_far, hi, lo = lax.optimization_barrier((c_near, c_far, hi, lo))

    def corners(start):
        pick = lambda x: lax.dynamic_slice_in_dim(x, start, H1, 0)
        return jnp.concatenate([pick(c_near), pick(c_far)], axis=1)

    odd_s = odd("src")
    x_near, x_far = exchange(
        corners((1 - odd_s) * (rows - H1)), corners(odd_s * (rows - H1)), "src"
    )
    grad = call(
        own_kernel,
        [hi, lo, cost_tgt],
        [((rows, cols), f32)],
        [],
        flops=4 * rows * cols * cols,
        moved=10 * MIB,
    )
    kernel, totals = call(
        tail_kernel,
        [c_near, c_far, x_near, x_far, cost_src, cost_tgt, grad, masked],
        [((rows, cols), f32), ((n_tgt, rows), f32)],
        [VMEM((rows, 2 * H2), bf16)] * 2 + [VMEM((rows, LANES), f32)],
        flops=2 * rows * 2 * H2 * (3 * cols + 2 * H1),
        moved=16 * MIB,
        exps=rows * cols,
    )
    row_totals = lax.all_to_all(totals, "tgt", 0, 0, tiled=True)
    scaled, totals = call(
        lambda *refs: column_kernel(float(cols * n_tgt), *refs),
        [row_totals, mass_src[None, :], kernel],
        [((rows, cols), f32), ((n_src, cols), f32)],
        [],
        moved=8 * MIB,
    )
    col_totals = lax.all_to_all(totals, "src", 0, 0, tiled=True)
    return call(
        lambda *refs: last_kernel(float(rows * n_src), *refs),
        [col_totals, mass_tgt[None, :], scaled],
        [jax.ShapeDtypeStruct((rows, cols), f32)],
        [VMEM((rows, cols), f32), dma((8,))],
        moved=8 * MIB,
    )


def solution(mesh):
    return jax.shard_map(
        per_device,
        mesh=mesh,
        in_specs=(
            P("src", "tgt"),
            P("src", None),
            P("tgt", None),
            P("src", "tgt"),
            P("src"),
            P("tgt"),
        ),
        out_specs=P("src", "tgt"),
        check_vma=False,
    )
```

time: 170 us -> 75 us (0.44)
  blocking collectives: 88.8 us -> 32.4 us
  matrix products: 24.7 us -> 0 us
  Pallas kernels: 0 us -> 20.5 us
  waiting for transfers between devices: 26.3 us -> 7.78 us
  other arithmetic: 11.5 us -> 0.04 us
  starting transfers between devices: 11.7 us -> 9.38 us
  local copies, waits for them, and re-layouts: 6.53 us -> 4.43 us
    psum x2 -> x0, blocking collectives: 88.8 us -> none  [the longest x1 61.4 us: per_device(): row_total = lax.psum(jnp.sum(kernel, axis=1), 'tgt')]
    all_to_all x0 -> x2, blocking collectives: none -> 32.4 us  [the longest x1 22.3 us: per_device(): row_totals = lax.all_to_all(totals, 'tgt', 0, 0, tiled=True)]
    dot_general x2 -> x0, matrix products: 24.7 us -> none  [the longest x1 21.3 us: per_device(): lax.dot_general(wide_product, cost_tgt.astype(jnp.float32), (((1,), (1,))...]
    pallas_call x0 -> x6, Pallas kernels: none -> 20.5 us  [call(): pl.pallas_call(body, out_shape=shapes[0] if single else shapes, in_specs=...]
    ppermute x4 -> x6, waiting for transfers between devices: 26.3 us -> 7.78 us  [exchange(): return (lax.ppermute(first, axis, near), lax.ppermute(second, axis, far))]
    mul x3 -> x0, other arithmetic: 8.14 us -> none  [the longest x1 4.61 us: per_device(): scaled * (mass_tgt * (row_count * lax.axis_size('src')) / col_total)[None...]
    reshape x1 -> x0, local copies, waits for them, and re-layouts: 4.61 us -> none  [per_device(): coupling.reshape(pattern.shape[0], TILE, pattern.shape[1], TILE)]
    unnamed x13 -> x16, local copies, waits for them, and re-layouts: 0.7 us -> 4.22 us
  transfers between devices with their start and end apart: 4 -> 6, of which waited for: 4 -> 2; matrix products, arithmetic and copies ran while one was open for 1% -> 0% of each run, Pallas kernels for 0% -> 14%
where the time goes in v2:
time: 75 us; the launch traced here: 74.7 us
  blocking collectives  32.4 us (43%)
  Pallas kernels  20.5 us (27%)
  starting transfers between devices  9.38 us (13%)
  waiting for transfers between devices  7.78 us (10%)
  local copies, waits for them, and re-layouts  4.43 us (6%)
    all_to_all x1, blocking collectives, per_device(): row_totals = lax.all_to_all(totals, 'tgt', 0, 0, tiled=True)  22.3 us
    pallas_call x6, Pallas kernels, call(): pl.pallas_call(body, out_shape=shapes[0] if single else shapes, in_specs=...  20.5 us
    all_to_all x1, blocking collectives, per_device(): col_totals = lax.all_to_all(totals, 'src', 0, 0, tiled=True)  10.1 us
    ppermute x6, starting transfers between devices, exchange(): return (lax.ppermute(first, axis, near), lax.ppermute(second, axis, far))  9.38 us
    ppermute x6, waiting for transfers between devices, exchange(): return (lax.ppermute(first, axis, near), lax.ppermute(second, axis, far))  7.78 us
    unnamed x16, local copies, waits for them, and re-layouts  4.22 us
  transfers between devices with their start and end apart: 6, of which 2 were waited for; matrix products, arithmetic and copies ran while one was open for 0% of the time, Pallas kernels for 14%

profile of v2, /device:TPU:1, one launch (start us, length us, event | category | flops | bytes accessed | tf_op | source)
XLA Modules:
  0.0 74.7 jit_solution(2702020543174244837)
XLA Ops:
  0.0 1.6 %copy-done.3 = bf16[1024,1024]{1,0:T(8,128)(2,1)S(1)} copy-done((bf16[1024,1024]{1,0:T(8,128)(2,1)S(1)}, bf16[1024,1024]{1,0:T(8,128)(2,1)}, u32[]{:S(2)}) %copy-start.3) | copy-done | bytes 2097176
  1.6 0.7 copy-done.6
  2.3 2.4 %shard_map.64 = (bf16[1024,1024]{1,0:T(8,128)(2,1)S(1)}, bf16[1024,256]{1,0:T(8,128)(2,1)}, bf16[1024,256]{1,0:T(8,128)(2,1)}, bf16[256,1024]{1,0:T(8,128)(2,1)}, bf16[256,1024]{1,0:T(8,128)(2,1)}) custom-call(s32[4,4]{1,0:T(4,128)S(1)} %copy-done.6, bf16[1024,1024]{1,0:T(8,128)(2,1)S(1)} %copy-done.3), custom_call_target="tpu_custom_call" | custom-call | bytes 6291456 | tf_op jit(solution)/shard_map/pallas_call | solution.py:167
  4.7 3.3 %collective-permute-start.2 = (bf16[256,1024]{1,0:T(8,128)(2,1)}, bf16[256,1024]{1,0:T(8,128)(2,1)}, u32[]{:S(2)}, u32[]{:S(2)}) collective-permute-start(bf16[256,1024]{1,0:T(8,128)(2,1)} %get-tuple-element.23), channel_id=1, source_target_pairs={{0,32},{32,0},{64,96},{96,64},{128,160},{160,128},{192,224},{224,1... | collective-permute-start | bytes 1572872 | tf_op jit(solution)/shard_map/ppermute | solution.py:188
  8.0 1.9 %collective-permute-start.3 = (bf16[256,1024]{1,0:T(8,128)(2,1)}, bf16[256,1024]{1,0:T(8,128)(2,1)}, u32[]{:S(2)}, u32[]{:S(2)}) collective-permute-start(bf16[256,1024]{1,0:T(8,128)(2,1)} %get-tuple-element.24), channel_id=1, source_target_pairs={{32,64},{64,32},{96,128},{128,96},{160,192},{192,160},{33,65},{65,... | collective-permute-start | bytes 1572872 | tf_op jit(solution)/shard_map/ppermute | solution.py:188
  9.9 1.2 %collective-permute-start = (bf16[1024,256]{1,0:T(8,128)(2,1)}, bf16[1024,256]{1,0:T(8,128)(2,1)S(1)}, u32[]{:S(2)}, u32[]{:S(2)}) collective-permute-start(bf16[1024,256]{1,0:T(8,128)(2,1)} %get-tuple-element.20), channel_id=1, source_target_pairs={{0,1},{1,0},{2,3},{3,2},{4,5},{5,4},{6,7},{7,6},{8,9},{9,8},{10,11... | collective-permute-start | bytes 1572872 | tf_op jit(solution)/shard_map/ppermute | solution.py:188
  11.1 0.7 collective-permute-start.1
  11.8 0.0 collective-permute-done.2.r_near
  11.8 7.2 %collective-permute-done.3.r_far = bf16[256,1024]{1,0:T(8,128)(2,1)} collective-permute-done((bf16[256,1024]{1,0:T(8,128)(2,1)}, bf16[256,1024]{1,0:T(8,128)(2,1)}, u32[]{:S(2)}, u32[]{:S(2)}) %collective-permute-start.3) | collective-permute-done | bytes 524320 | tf_op jit(solution)/shard_map/ppermute | solution.py:188
  19.0 1.9 %copy-done = bf16[1024,1536]{1,0:T(8,128)(2,1)S(1)} copy-done((bf16[1024,1536]{1,0:T(8,128)(2,1)S(1)}, bf16[1024,1536]{1,0:T(8,128)(2,1)}, u32[]{:S(2)}) %copy-start) | copy-done | bytes 3145752
  20.9 5.3 %shard_map.65 = (bf16[1024,1024]{1,0:T(8,128)(2,1)S(1)}, bf16[1024,1024]{1,0:T(8,128)(2,1)S(1)}) custom-call(bf16[1024,1024]{1,0:T(8,128)(2,1)S(1)} %get-tuple-element.22.masked, bf16[256,1024]{1,0:T(8,128)(2,1)} %collective-permute-done.2.r_near, bf16[256,1024]{1,0:T(8,128)(2,1)} %collective-permute-done.3.r_far, bf16[1024,1536]{1,0:T(8,128)(2,1)S(1)} %copy-done), custom_call_target="tpu_custom_call" | custom-call | flops 3221225472 | bytes 10485760 | tf_op jit(solution)/shard_map/pallas_call | solution.py:167
  26.3 0.1 collective-permute-start.4
  26.5 0.0 copy-start.1
  26.5 2.2 %collective-permute-start.5 = (bf16[256,512]{1,0:T(8,128)(2,1)S(1)}, bf16[256,512]{1,0:T(8,128)(2,1)S(1)}, u32[]{:S(2)}, u32[]{:S(2)}) collective-permute-start(bf16[256,512]{1,0:T(8,128)(2,1)S(1)} %pad_maximum_fusion.1), channel_id=1, source_target_pairs={{32,64},{64,32},{96,128},{128,96},{160,192},{192,160},{33,65},{65,... | collective-permute-start | bytes 786440 | tf_op jit(solution)/shard_map/ppermute | solution.py:188
  28.7 5.1 %shard_map.66.grad = f32[1024,1024]{1,0:T(8,128)S(1)} custom-call(bf16[1024,1024]{1,0:T(8,128)(2,1)S(1)} %get-tuple-element.29.hi, bf16[1024,1024]{1,0:T(8,128)(2,1)S(1)} %get-tuple-element.30.lo, bf16[1024,1536]{1,0:T(8,128)(2,1)S(1)} %copy-done.2), custom_call_target="tpu_custom_call" | custom-call | flops 4294967296 | bytes 10485760 | tf_op jit(solution)/shard_map/pallas_call | solution.py:167
  33.8 0.0 copy-start.4
  33.8 0.6 collective-permute-done.5.x_far
  34.4 5.1 %shard_map.67 = (f32[1024,1024]{1,0:T(8,128)S(1)}, f32[32,1024]{1,0:T(8,128)S(1)}) custom-call(bf16[1024,256]{1,0:T(8,128)(2,1)S(1)} %collective-permute-done.c_near, bf16[1024,256]{1,0:T(8,128)(2,1)S(1)} %collective-permute-done.1.c_far, bf16[256,512]{1,0:T(8,128)(2,1)S(1)} %collective-permute-done.4.x_near, ...), custom_call_target="tpu_custom_call" | custom-call | flops 3758096384 | bytes 16777216 | tf_op jit(solution)/shard_map/pallas_call | solution.py:167
  39.5 0.0 copy-start.5
  39.5 0.1 copy.7
  39.6 22.3 %all_to_all.22 = f32[32,1,1024]{2,1,0:T(1,128)S(1)} all-to-all(f32[32,1,1024]{2,1,0:T(1,128)S(1)} %copy.7), channel_id=1, replica_groups=mesh['src'=8,'tgt'=32] {'tgt'}, dimensions={0} | all-to-all | bytes 262144 | tf_op jit(solution)/shard_map/all_to_all | solution.py:242
  62.0 0.5 shard_map.68
  62.5 10.1 %all_to_all.23 = f32[8,1,1024]{2,1,0:T(1,128)S(1)} all-to-all(f32[8,1,1024]{2,1,0:T(1,128)S(1)} %copy.8), channel_id=1, replica_groups=mesh['src'=8,'tgt'=32] {'src'}, dimensions={0} | all-to-all | bytes 65536 | tf_op jit(solution)/shard_map/all_to_all | solution.py:250
  72.6 2.1 %shard_map.69 = f32[1024,1024]{1,0:T(8,128)} custom-call(f32[8,1024]{1,0:T(8,128)S(1)} %bitcast.11, f32[1,1024]{1,0:T(1,128)S(1)} %bitcast.15, f32[1024,1024]{1,0:T(8,128)S(1)} %get-tuple-element.34.refs_2_), custom_call_target="tpu_custom_call" | custom-call | bytes 8388608 | tf_op jit(solution)/shard_map/pallas_call | solution.py:167
  (17 shorter events, 0.2 us)
Async XLA Ops:
  0.0 1.6 %copy-start.3 = (bf16[1024,1024]{1,0:T(8,128)(2,1)S(1)}, bf16[1024,1024]{1,0:T(8,128)(2,1)}, u32[]{:S(2)}) copy-start(bf16[1024,1024]{1,0:T(8,128)(2,1)} %coupling.1) | copy-start | bytes 6291460
  1.6 0.7 copy-start.6
  4.7 7.1 %collective-permute-start.2 = (bf16[256,1024]{1,0:T(8,128)(2,1)}, bf16[256,1024]{1,0:T(8,128)(2,1)}, u32[]{:S(2)}, u32[]{:S(2)}) collective-permute-start(bf16[256,1024]{1,0:T(8,128)(2,1)} %get-tuple-element.23), channel_id=1, source_target_pairs={{0,32},{32,0},{64,96},{96,64},{128,160},{160,128},{192,224},{224,1... | collective-permute-start | bytes 1572872 | tf_op jit(solution)/shard_map/ppermute | solution.py:188
  8.0 11.0 %collective-permute-start.3 = (bf16[256,1024]{1,0:T(8,128)(2,1)}, bf16[256,1024]{1,0:T(8,128)(2,1)}, u32[]{:S(2)}, u32[]{:S(2)}) collective-permute-start(bf16[256,1024]{1,0:T(8,128)(2,1)} %get-tuple-element.24), channel_id=1, source_target_pairs={{32,64},{64,32},{96,128},{128,96},{160,192},{192,160},{33,65},{65,... | collective-permute-start | bytes 1572872 | tf_op jit(solution)/shard_map/ppermute | solution.py:188
  9.9 16.3 %collective-permute-start = (bf16[1024,256]{1,0:T(8,128)(2,1)}, bf16[1024,256]{1,0:T(8,128)(2,1)S(1)}, u32[]{:S(2)}, u32[]{:S(2)}) collective-permute-start(bf16[1024,256]{1,0:T(8,128)(2,1)} %get-tuple-element.20), channel_id=1, source_target_pairs={{0,1},{1,0},{2,3},{3,2},{4,5},{5,4},{6,7},{7,6},{8,9},{9,8},{10,11... | collective-permute-start | bytes 1572872 | tf_op jit(solution)/shard_map/ppermute | solution.py:188
  11.1 15.1 %collective-permute-start.1 = (bf16[1024,256]{1,0:T(8,128)(2,1)}, bf16[1024,256]{1,0:T(8,128)(2,1)S(1)}, u32[]{:S(2)}, u32[]{:S(2)}) collective-permute-start(bf16[1024,256]{1,0:T(8,128)(2,1)} %get-tuple-element.21), channel_id=1, source_target_pairs={{1,2},{2,1},{3,4},{4,3},{5,6},{6,5},{7,8},{8,7},{9,10},{10,9},{11,... | collective-permute-start | bytes 1572872 | tf_op jit(solution)/shard_map/ppermute | solution.py:188
  19.0 1.9 %copy-start = (bf16[1024,1536]{1,0:T(8,128)(2,1)S(1)}, bf16[1024,1536]{1,0:T(8,128)(2,1)}, u32[]{:S(2)}) copy-start(bf16[1024,1536]{1,0:T(8,128)(2,1)} %cost_src.3) | copy-start | bytes 9437188
  20.9 7.7 %copy-start.2 = (bf16[1024,1536]{1,0:T(8,128)(2,1)S(1)}, bf16[1024,1536]{1,0:T(8,128)(2,1)}, u32[]{:S(2)}) copy-start(bf16[1024,1536]{1,0:T(8,128)(2,1)} %cost_tgt.3) | copy-start | bytes 9437188
  26.3 7.5 %collective-permute-start.4 = (bf16[256,512]{1,0:T(8,128)(2,1)S(1)}, bf16[256,512]{1,0:T(8,128)(2,1)S(1)}, u32[]{:S(2)}, u32[]{:S(2)}) collective-permute-start(bf16[256,512]{1,0:T(8,128)(2,1)S(1)} %pad_maximum_fusion), channel_id=1, source_target_pairs={{0,32},{32,0},{64,96},{96,64},{128,160},{160,128},{192,224},{224,1... | collective-permute-start | bytes 786440 | tf_op jit(solution)/shard_map/ppermute | solution.py:188
  26.5 8.0 %copy-start.1 = (bf16[1024,1536]{1,0:T(8,128)(2,1)S(1)}, bf16[1024,1536]{1,0:T(8,128)(2,1)}, u32[]{:S(2)}) copy-start(bf16[1024,1536]{1,0:T(8,128)(2,1)} %cost_src.3) | copy-start | bytes 9437188
  26.5 8.0 %collective-permute-start.5 = (bf16[256,512]{1,0:T(8,128)(2,1)S(1)}, bf16[256,512]{1,0:T(8,128)(2,1)S(1)}, u32[]{:S(2)}, u32[]{:S(2)}) collective-permute-start(bf16[256,512]{1,0:T(8,128)(2,1)S(1)} %pad_maximum_fusion.1), channel_id=1, source_target_pairs={{32,64},{64,32},{96,128},{128,96},{160,192},{192,160},{33,65},{65,... | collective-permute-start | bytes 786440 | tf_op jit(solution)/shard_map/ppermute | solution.py:188
  33.8 28.2 %copy-start.4 = (f32[1024]{0:T(1024)S(1)}, f32[1024]{0:T(1024)}, u32[]{:S(2)}) copy-start(f32[1024]{0:T(1024)} %param.10) | copy-start | bytes 12292
  39.5 33.1 %copy-start.5 = (f32[1024]{0:T(1024)S(1)}, f32[1024]{0:T(1024)}, u32[]{:S(2)}) copy-start(f32[1024]{0:T(1024)} %param.11) | copy-start | bytes 12292

commit v3 on v2

v3 whole, which is shorter than its diff:
```python
import jax
import jax.numpy as jnp
from jax import lax
from jax.experimental import pallas as pl
from jax.experimental.pallas import tpu as pltpu
from jax.sharding import PartitionSpec as P

TILE = 256
H1 = 256
H2 = 256
LANES = 128

step_size = 1.0

f32 = jnp.float32
bf16 = jnp.bfloat16
VMEM = pltpu.VMEM
MIB = 1 << 20


def odd(axis):
    return lax.rem(lax.axis_index(axis), 2) == 1


def dot(a, b):
    return jnp.dot(a, b, preferred_element_type=f32)


def dot_t(a, b):
    return lax.dot_general(a, b, (((1,), (1,)), ((), ())), preferred_element_type=f32)


def halves(x):
    hi = x.astype(bf16)
    return hi, (x - hi.astype(f32)).astype(bf16)


def as_row(x):
    return jnp.sum(x.T, axis=0, keepdims=True)


def tiles_of(size):
    return [slice(n * TILE, (n + 1) * TILE) for n in range(size // TILE)]


def side_kernel(pattern, coupling, masked, c_near, c_far, raw, gates, sems, sem):
    rows, cols = masked.shape
    down, along = tiles_of(rows), tiles_of(cols)
    gate = pltpu.make_async_copy(pattern, gates, sem)
    copies = [
        pltpu.make_async_copy(coupling.at[part], raw.at[part], sems.at[r])
        for r, part in enumerate(down)
    ]
    for copy in copies:
        copy.start()
    gate.start()
    odd_t = odd("tgt")
    gate.wait()
    for r, part in enumerate(down):
        copies[r].wait()
        for c, across in enumerate(along):
            tile = raw[part, across]
            masked[part, across] = jnp.where(gates[r, c] != 0, tile, jnp.zeros_like(tile))
        first, last = masked[part, along[0]], masked[part, along[-1]]
        c_near[part, :] = jnp.where(odd_t, first, last)
        c_far[part, :] = jnp.where(odd_t, last, first)


def band_copies(band, own, width, parity, out, sems):
    last = own + width
    near = pl.multiple_of((1 - parity) * last, TILE)
    far = pl.multiple_of(parity * last, TILE)
    spans = [(width, own, 0), (near, width, own), (far, width, own + width)]
    return [
        pltpu.make_async_copy(
            band.at[:, pl.ds(start, size)], out.at[:, pl.ds(to, size)], sems.at[n]
        )
        for n, (start, size, to) in enumerate(spans)
    ]


def end_kernel(masked, src_hbm, r_near, r_far, cost_src, sems):
    rows, cols = masked.shape
    copies = band_copies(src_hbm, rows, H1, odd("src").astype(jnp.int32), cost_src, sems)
    for copy in copies:
        copy.start()
    first, last = masked[:H1, :], masked[rows - H1:, :]
    odd_s = odd("src")
    r_near[...] = jnp.where(odd_s, first, last)
    r_far[...] = jnp.where(odd_s, last, first)
    for copy in copies:
        copy.wait()


def local_kernel(masked, cost_src, tgt_hbm, grad, cost_tgt, hi, lo, sems):
    rows, cols = masked.shape
    copies = band_copies(tgt_hbm, cols, H2, odd("tgt").astype(jnp.int32), cost_tgt, sems)
    for copy in copies:
        copy.start()
    for across in tiles_of(cols):
        hi[:, across], lo[:, across] = halves(dot(cost_src[:, :rows], masked[:, across]))
    for copy in copies:
        copy.wait()
    for across in tiles_of(cols):
        costs = cost_tgt[across, :cols]
        both = jnp.concatenate([hi[...], lo[...]], axis=1)
        grad[:, across] = dot_t(both, jnp.concatenate([costs, costs], axis=1))


def corner_kernel(c_near, c_far, x_near, x_far):
    rows = c_near.shape[0]
    odd_s = odd("src")
    for n, side in enumerate((c_near, c_far)):
        across = slice(n * H2, (n + 1) * H2)
        first, last = side[:H1, :], side[rows - H1:, :]
        x_near[:, across] = jnp.where(odd_s, first, last)
        x_far[:, across] = jnp.where(odd_s, last, first)


def halo_kernel(c_near, c_far, r_near, r_far, cost_src, cost_tgt, grad,
                out, ends, hi, lo):
    rows, cols = grad.shape
    for n, side in enumerate((c_near, c_far)):
        across = slice(n * H2, (n + 1) * H2)
        hi[:, across], lo[:, across] = halves(dot(cost_src[:, :rows], side[...]))
    for across in tiles_of(cols):
        costs = cost_tgt[across, cols:]
        both = jnp.concatenate([hi[...], lo[...]], axis=1)
        out[:, across] = grad[:, across] + dot_t(both, jnp.concatenate([costs, costs], axis=1))
    rim = jnp.concatenate([r_near[...], r_far[...]], axis=0)
    for across in tiles_of(cols):
        ends[:, across] = dot_t(rim, cost_tgt[across, :cols])


def tail_kernel(x_near, x_far, cost_src, cost_tgt, ends, grad, masked, kernel, totals, part):
    rows, cols = masked.shape
    corners = jnp.concatenate([x_near[...], x_far[...]], axis=0)
    bands = cost_src[:, rows:]
    bands = jnp.concatenate([bands, bands], axis=1)
    for n, across in enumerate(tiles_of(cols)):
        hi, lo = halves(ends[:, across] + dot_t(corners, cost_tgt[across, cols:]))
        slope = grad[:, across] + dot(bands, jnp.concatenate([hi, lo], axis=0))
        value = masked[:, across].astype(f32) * jnp.exp(step_size * slope)
        kernel[:, across] = value
        sums = value[:, :LANES] + value[:, LANES:]
        part[...] = sums if n == 0 else part[...] + sums
    totals[...] = jnp.broadcast_to(as_row(part[...]), totals.shape)


def column_kernel(total, row_totals, mass, kernel, scaled, totals):
    rows, cols = kernel.shape
    factor = mass[...] * total / jnp.sum(row_totals[...], axis=0, keepdims=True)
    factor = jnp.broadcast_to(factor, (LANES, rows)).T
    for n in range(cols // LANES):
        across = slice(n * LANES, (n + 1) * LANES)
        value = kernel[:, across] * factor
        scaled[:, across] = value
        sums = jnp.sum(value, axis=0, keepdims=True)
        totals[:, across] = jnp.broadcast_to(sums, (totals.shape[0], LANES))


def last_kernel(total, col_totals, mass, scaled, out, block, sems):
    rows, cols = scaled.shape
    factor = mass[...] * total / jnp.sum(col_totals[...], axis=0, keepdims=True)
    n_blocks = sems.shape[0]
    size = rows // n_blocks

    def copy(n):
        part = pl.ds(n * size, size)
        return pltpu.make_async_copy(block.at[part], out.at[part], sems.at[n])

    for n in range(n_blocks):
        part = slice(n * size, (n + 1) * size)
        block[part, :] = scaled[part, :] * factor
        copy(n).start()
    for n in range(n_blocks):
        copy(n).wait()


def call(body, inputs, outputs, scratch, far=(), limit=12, flops=0, moved=0, exps=0):
    args, in_specs = [], []
    for n, x in enumerate(inputs):
        args.append(pltpu.with_memory_space_constraint(x, pltpu.HBM if n in far else VMEM))
        in_specs.append(pl.BlockSpec(memory_space=pl.ANY if n in far else VMEM))
    is_far = [isinstance(s, jax.ShapeDtypeStruct) for s in outputs]
    shapes = [s if f else VMEM(*s) for s, f in zip(outputs, is_far)]
    out_specs = [pl.BlockSpec(memory_space=pl.ANY if f else VMEM) for f in is_far]
    single = len(outputs) == 1
    return pl.pallas_call(
        body,
        out_shape=shapes[0] if single else shapes,
        in_specs=in_specs,
        out_specs=out_specs[0] if single else out_specs,
        scratch_shapes=scratch,
        cost_estimate=pl.CostEstimate(flops=flops, bytes_accessed=moved, transcendentals=exps),
        compiler_params=pltpu.CompilerParams(vmem_limit_bytes=limit * MIB),
    )(*args)


def pair_plans(size):
    near = [(i, i ^ 1) for i in range(size)]
    far = []
    for i in range(1, size - 1, 2):
        far += [(i, i + 1), (i + 1, i)]
    return near, far


def exchange(first, second, axis):
    near, far = pair_plans(lax.axis_size(axis))
    return lax.ppermute(first, axis, near), lax.ppermute(second, axis, far)


def per_device(coupling, cost_src, cost_tgt, pattern, mass_src, mass_tgt):
    rows, cols = coupling.shape
    n_src, n_tgt = lax.axis_size("src"), lax.axis_size("tgt")
    tiles = pattern.shape[0]
    dma = pltpu.SemaphoreType.DMA

    masked, c_near, c_far = call(
        side_kernel,
        [pattern, coupling],
        [((rows, cols), bf16)] + [((rows, H2), bf16)] * 2,
        [
            VMEM((rows, cols), bf16),
            pltpu.SMEM(pattern.shape, pattern.dtype),
            dma((tiles,)),
            dma,
        ],
        far=(0, 1),
        moved=6 * MIB,
    )
    c_near, c_far = exchange(c_near, c_far, "tgt")
    r_near, r_far, cost_src = call(
        end_kernel,
        [masked, cost_src],
        [((H1, cols), bf16)] * 2 + [(cost_src.shape, bf16)],
        [dma((3,))],
        far=(1,),
        moved=5 * MIB,
    )
    r_near, r_far = exchange(r_near, r_far, "src")
    grad, cost_tgt = call(
        local_kernel,
        [masked, cost_src, cost_tgt],
        [((rows, cols), f32), (cost_tgt.shape, bf16)],
        [VMEM((rows, cols), bf16)] * 2 + [dma((3,))],
        far=(2,),
        moved=MIB,
    )

    x_near, x_far = call(
        corner_kernel,
        [c_near, c_far],
        [((H1, 2 * H2), bf16)] * 2,
        [],
        moved=1024 * MIB,
    )
    x_near, x_far = exchange(x_near, x_far, "src")
    grad, ends = call(
        halo_kernel,
        [c_near, c_far, r_near, r_far, cost_src, cost_tgt, grad],
        [((rows, cols), f32), ((2 * H1, cols), f32)],
        [VMEM((rows, 2 * H2), bf16)] * 2,
        flops=2 * rows * cols * (2 * H1 + 6 * H2),
        moved=10 * MIB,
    )
    kernel, totals = call(
        tail_kernel,
        [x_near, x_far, cost_src, cost_tgt, ends, grad, masked],
        [((rows, cols), f32), ((n_tgt, rows), f32)],
        [VMEM((rows, LANES), f32)],
        flops=2 * rows * cols * (4 * H1 + H2),
        moved=16 * MIB,
        exps=rows * cols,
    )
    row_totals = lax.all_to_all(totals, "tgt", 0, 0, tiled=True)
    scaled, totals = call(
        lambda *refs: column_kernel(float(cols * n_tgt), *refs),
        [row_totals, mass_src[None, :], kernel],
        [((rows, cols), f32), ((n_src, cols), f32)],
        [],
        moved=8 * MIB,
    )
    col_totals = lax.all_to_all(totals, "src", 0, 0, tiled=True)
    return call(
        lambda *refs: last_kernel(float(rows * n_src), *refs),
        [col_totals, mass_tgt[None, :], scaled],
        [jax.ShapeDtypeStruct((rows, cols), f32)],
        [VMEM((rows, cols), f32), dma((8,))],
        moved=8 * MIB,
    )


def solution(mesh):
    return jax.shard_map(
        per_device,
        mesh=mesh,
        in_specs=(
            P("src", "tgt"),
            P("src", None),
            P("tgt", None),
            P("src", "tgt"),
            P("src"),
            P("tgt"),
        ),
        out_specs=P("src", "tgt"),
        check_vma=False,
    )
```

time: 75 us -> 67.2 us (0.90)
  waiting for transfers between devices: 7.78 us -> 0.02 us
  local copies, waits for them, and re-layouts: 4.43 us -> 0.22 us
  Pallas kernels: 20.5 us -> 23.3 us
  starting transfers between devices: 9.38 us -> 11.2 us
    ppermute x6, waiting for transfers between devices: 7.78 us -> 0.02 us  [exchange(): return (lax.ppermute(first, axis, near), lax.ppermute(second, axis, far))]
    unnamed x16 -> x6, local copies, waits for them, and re-layouts: 4.22 us -> 0.04 us
    pallas_call x6 -> x8, Pallas kernels: 20.5 us -> 23.3 us  [call(): pl.pallas_call(body, out_shape=shapes[0] if single else shapes, in_specs=...]
    ppermute x6, starting transfers between devices: 9.38 us -> 11.2 us  [exchange(): return (lax.ppermute(first, axis, near), lax.ppermute(second, axis, far))]
    all_to_all x1, blocking collectives: 22.3 us -> 20.9 us  [per_device(): row_totals = lax.all_to_all(totals, 'tgt', 0, 0, tiled=True)]
    all_to_all x1, blocking collectives: 10.1 us -> 10.9 us  [per_device(): col_totals = lax.all_to_all(totals, 'src', 0, 0, tiled=True)]
  transfers between devices with their start and end apart: 6 -> 6, of which waited for: 2 -> 0; matrix products, arithmetic and copies ran while one was open for 0% -> 0% of each run, Pallas kernels for 14% -> 22%
where the time goes in v3:
time: 67.2 us; the launch traced here: 66.9 us
  blocking collectives  31.9 us (47%)
  Pallas kernels  23.3 us (35%)
  starting transfers between devices  11.2 us (17%)
    pallas_call x8, Pallas kernels, call(): pl.pallas_call(body, out_shape=shapes[0] if single else shapes, in_specs=...  23.3 us
    all_to_all x1, blocking collectives, per_device(): row_totals = lax.all_to_all(totals, 'tgt', 0, 0, tiled=True)  20.9 us
    ppermute x6, starting transfers between devices, exchange(): return (lax.ppermute(first, axis, near), lax.ppermute(second, axis, far))  11.2 us
    all_to_all x1, blocking collectives, per_device(): col_totals = lax.all_to_all(totals, 'src', 0, 0, tiled=True)  10.9 us
  transfers between devices with their start and end apart: 6, of which 0 were waited for; matrix products, arithmetic and copies ran while one was open for 0% of the time, Pallas kernels for 22%

profile of v3, /device:TPU:1, one launch (start us, length us, event | category | flops | bytes accessed | tf_op | source)
XLA Modules:
  0.0 66.9 jit_solution(17579250625609708337)
XLA Ops:
  0.0 1.6 %shard_map.64 = (bf16[1024,1024]{1,0:T(8,128)(2,1)S(1)}, bf16[1024,256]{1,0:T(8,128)(2,1)S(1)}, bf16[1024,256]{1,0:T(8,128)(2,1)S(1)}) custom-call(s32[4,4]{1,0:T(4,128)} %pattern.1, bf16[1024,1024]{1,0:T(8,128)(2,1)} %coupling.1), custom_call_target="tpu_custom_call" | custom-call | bytes 6291456 | tf_op jit(solution)/shard_map/pallas_call | solution.py:189
  1.6 2.6 %collective-permute-start = (bf16[1024,256]{1,0:T(8,128)(2,1)S(1)}, bf16[1024,256]{1,0:T(8,128)(2,1)S(1)}, u32[]{:S(2)}, u32[]{:S(2)}) collective-permute-start(bf16[1024,256]{1,0:T(8,128)(2,1)S(1)} %get-tuple-element.21), channel_id=1, source_target_pairs={{0,1},{1,0},{2,3},{3,2},{4,5},{5,4},{6,7},{7,6},{8,9},{9,8},{10,11... | collective-permute-start | bytes 1572872 | tf_op jit(solution)/shard_map/ppermute | solution.py:210
  4.2 0.7 %collective-permute-start.1 = (bf16[1024,256]{1,0:T(8,128)(2,1)S(1)}, bf16[1024,256]{1,0:T(8,128)(2,1)S(1)}, u32[]{:S(2)}, u32[]{:S(2)}) collective-permute-start(bf16[1024,256]{1,0:T(8,128)(2,1)S(1)} %get-tuple-element.22), channel_id=1, source_target_pairs={{1,2},{2,1},{3,4},{4,3},{5,6},{6,5},{7,8},{8,7},{9,10},{10,9},{11,... | collective-permute-start | bytes 1572872 | tf_op jit(solution)/shard_map/ppermute | solution.py:210
  4.9 1.9 %shard_map.66 = (bf16[256,1024]{1,0:T(8,128)(2,1)S(1)}, bf16[256,1024]{1,0:T(8,128)(2,1)S(1)}, bf16[1024,1536]{1,0:T(8,128)(2,1)S(1)}) custom-call(bf16[1024,1024]{1,0:T(8,128)(2,1)S(1)} %get-tuple-element.25.masked, bf16[1024,1536]{1,0:T(8,128)(2,1)} %src_hbm.1), custom_call_target="tpu_custom_call" | custom-call | bytes 5242880 | tf_op jit(solution)/shard_map/pallas_call | solution.py:189
  6.7 1.0 %collective-permute-start.4 = (bf16[256,1024]{1,0:T(8,128)(2,1)S(1)}, bf16[256,1024]{1,0:T(8,128)(2,1)S(1)}, u32[]{:S(2)}, u32[]{:S(2)}) collective-permute-start(bf16[256,1024]{1,0:T(8,128)(2,1)S(1)} %get-tuple-element.28), channel_id=1, source_target_pairs={{0,32},{32,0},{64,96},{96,64},{128,160},{160,128},{192,224},{224,1... | collective-permute-start | bytes 1572872 | tf_op jit(solution)/shard_map/ppermute | solution.py:210
  7.8 3.1 %collective-permute-start.5 = (bf16[256,1024]{1,0:T(8,128)(2,1)S(1)}, bf16[256,1024]{1,0:T(8,128)(2,1)S(1)}, u32[]{:S(2)}, u32[]{:S(2)}) collective-permute-start(bf16[256,1024]{1,0:T(8,128)(2,1)S(1)} %get-tuple-element.29), channel_id=1, source_target_pairs={{32,64},{64,32},{96,128},{128,96},{160,192},{192,160},{33,65},{65,... | collective-permute-start | bytes 1572872 | tf_op jit(solution)/shard_map/ppermute | solution.py:210
  10.9 8.3 %shard_map.67 = (f32[1024,1024]{1,0:T(8,128)S(1)}, bf16[1024,1536]{1,0:T(8,128)(2,1)S(1)}) custom-call(bf16[1024,1024]{1,0:T(8,128)(2,1)S(1)} %get-tuple-element.25.masked, bf16[1024,1536]{1,0:T(8,128)(2,1)S(1)} %get-tuple-element.26.cost_src, bf16[1024,1536]{1,0:T(8,128)(2,1)} %tgt_hbm.1), custom_call_target="tpu_custom_call" | custom-call | bytes 1048576 | tf_op jit(solution)/shard_map/pallas_call | solution.py:189
  19.2 0.0 collective-permute-done.c_near
  19.2 0.0 collective-permute-done.1.c_far
  19.2 0.1 shard_map.65
  19.3 0.1 collective-permute-start.2
  19.4 3.8 %collective-permute-start.3 = (bf16[256,512]{1,0:T(8,128)(2,1)S(1)}, bf16[256,512]{1,0:T(8,128)(2,1)S(1)}, u32[]{:S(2)}, u32[]{:S(2)}) collective-permute-start(bf16[256,512]{1,0:T(8,128)(2,1)S(1)} %get-tuple-element.24), channel_id=1, source_target_pairs={{32,64},{64,32},{96,128},{128,96},{160,192},{192,160},{33,65},{65,... | collective-permute-start | bytes 786440 | tf_op jit(solution)/shard_map/ppermute | solution.py:210
  23.2 0.0 collective-permute-done.4.r_near
  23.2 0.0 collective-permute-done.5.r_far
  23.2 4.5 %shard_map.68 = (f32[1024,1024]{1,0:T(8,128)S(1)}, f32[512,1024]{1,0:T(8,128)S(1)}) custom-call(bf16[1024,256]{1,0:T(8,128)(2,1)S(1)} %collective-permute-done.c_near, bf16[1024,256]{1,0:T(8,128)(2,1)S(1)} %collective-permute-done.1.c_far, bf16[256,1024]{1,0:T(8,128)(2,1)S(1)} %collective-permute-done.4.r_near, ...), custom_call_target="tpu_custom_call" | custom-call | flops 4294967296 | bytes 10485760 | tf_op jit(solution)/shard_map/pallas_call | solution.py:189
  27.7 0.0 collective-permute-done.2.x_near
  27.7 0.0 copy-start
  27.7 4.3 %shard_map.69 = (f32[1024,1024]{1,0:T(8,128)S(1)}, f32[32,1024]{1,0:T(8,128)S(1)}) custom-call(bf16[256,512]{1,0:T(8,128)(2,1)S(1)} %collective-permute-done.2.x_near, bf16[256,512]{1,0:T(8,128)(2,1)S(1)} %collective-permute-done.3.x_far, bf16[1024,1536]{1,0:T(8,128)(2,1)S(1)} %get-tuple-element.26.cost_src, ...), custom_call_target="tpu_custom_call" | custom-call | flops 2684354560 | bytes 16777216 | tf_op jit(solution)/shard_map/pallas_call | solution.py:189
  32.0 0.0 copy-start.1
  32.0 0.1 copy.7
  32.2 20.9 %all_to_all.22 = f32[32,1,1024]{2,1,0:T(1,128)S(1)} all-to-all(f32[32,1,1024]{2,1,0:T(1,128)S(1)} %copy.7), channel_id=1, replica_groups=mesh['src'=8,'tgt'=32] {'tgt'}, dimensions={0} | all-to-all | bytes 262144 | tf_op jit(solution)/shard_map/all_to_all | solution.py:276
  53.2 0.5 shard_map.70
  53.7 10.9 %all_to_all.23 = f32[8,1,1024]{2,1,0:T(1,128)S(1)} all-to-all(f32[8,1,1024]{2,1,0:T(1,128)S(1)} %copy.8), channel_id=1, replica_groups=mesh['src'=8,'tgt'=32] {'src'}, dimensions={0} | all-to-all | bytes 65536 | tf_op jit(solution)/shard_map/all_to_all | solution.py:284
  64.6 2.1 %shard_map.71 = f32[1024,1024]{1,0:T(8,128)} custom-call(f32[8,1024]{1,0:T(8,128)S(1)} %bitcast.11, f32[1,1024]{1,0:T(1,128)S(1)} %bitcast.15, f32[1024,1024]{1,0:T(8,128)S(1)} %get-tuple-element.36.refs_2_), custom_call_target="tpu_custom_call" | custom-call | bytes 8388608 | tf_op jit(solution)/shard_map/pallas_call | solution.py:189
  (6 shorter events, 0.1 us)
Async XLA Ops:
  1.6 17.6 %collective-permute-start = (bf16[1024,256]{1,0:T(8,128)(2,1)S(1)}, bf16[1024,256]{1,0:T(8,128)(2,1)S(1)}, u32[]{:S(2)}, u32[]{:S(2)}) collective-permute-start(bf16[1024,256]{1,0:T(8,128)(2,1)S(1)} %get-tuple-element.21), channel_id=1, source_target_pairs={{0,1},{1,0},{2,3},{3,2},{4,5},{5,4},{6,7},{7,6},{8,9},{9,8},{10,11... | collective-permute-start | bytes 1572872 | tf_op jit(solution)/shard_map/ppermute | solution.py:210
  4.2 15.0 %collective-permute-start.1 = (bf16[1024,256]{1,0:T(8,128)(2,1)S(1)}, bf16[1024,256]{1,0:T(8,128)(2,1)S(1)}, u32[]{:S(2)}, u32[]{:S(2)}) collective-permute-start(bf16[1024,256]{1,0:T(8,128)(2,1)S(1)} %get-tuple-element.22), channel_id=1, source_target_pairs={{1,2},{2,1},{3,4},{4,3},{5,6},{6,5},{7,8},{8,7},{9,10},{10,9},{11,... | collective-permute-start | bytes 1572872 | tf_op jit(solution)/shard_map/ppermute | solution.py:210
  6.7 16.4 %collective-permute-start.4 = (bf16[256,1024]{1,0:T(8,128)(2,1)S(1)}, bf16[256,1024]{1,0:T(8,128)(2,1)S(1)}, u32[]{:S(2)}, u32[]{:S(2)}) collective-permute-start(bf16[256,1024]{1,0:T(8,128)(2,1)S(1)} %get-tuple-element.28), channel_id=1, source_target_pairs={{0,32},{32,0},{64,96},{96,64},{128,160},{160,128},{192,224},{224,1... | collective-permute-start | bytes 1572872 | tf_op jit(solution)/shard_map/ppermute | solution.py:210
  7.8 15.4 %collective-permute-start.5 = (bf16[256,1024]{1,0:T(8,128)(2,1)S(1)}, bf16[256,1024]{1,0:T(8,128)(2,1)S(1)}, u32[]{:S(2)}, u32[]{:S(2)}) collective-permute-start(bf16[256,1024]{1,0:T(8,128)(2,1)S(1)} %get-tuple-element.29), channel_id=1, source_target_pairs={{32,64},{64,32},{96,128},{128,96},{160,192},{192,160},{33,65},{65,... | collective-permute-start | bytes 1572872 | tf_op jit(solution)/shard_map/ppermute | solution.py:210
  19.3 8.4 %collective-permute-start.2 = (bf16[256,512]{1,0:T(8,128)(2,1)S(1)}, bf16[256,512]{1,0:T(8,128)(2,1)S(1)}, u32[]{:S(2)}, u32[]{:S(2)}) collective-permute-start(bf16[256,512]{1,0:T(8,128)(2,1)S(1)} %get-tuple-element.23), channel_id=1, source_target_pairs={{0,32},{32,0},{64,96},{96,64},{128,160},{160,128},{192,224},{224,1... | collective-permute-start | bytes 786440 | tf_op jit(solution)/shard_map/ppermute | solution.py:210
  19.4 8.3 %collective-permute-start.3 = (bf16[256,512]{1,0:T(8,128)(2,1)S(1)}, bf16[256,512]{1,0:T(8,128)(2,1)S(1)}, u32[]{:S(2)}, u32[]{:S(2)}) collective-permute-start(bf16[256,512]{1,0:T(8,128)(2,1)S(1)} %get-tuple-element.24), channel_id=1, source_target_pairs={{32,64},{64,32},{96,128},{128,96},{160,192},{192,160},{33,65},{65,... | collective-permute-start | bytes 786440 | tf_op jit(solution)/shard_map/ppermute | solution.py:210
  27.7 25.5 %copy-start = (f32[1024]{0:T(1024)S(1)}, f32[1024]{0:T(1024)}, u32[]{:S(2)}) copy-start(f32[1024]{0:T(1024)} %param.10) | copy-start | bytes 12292
  32.0 32.6 %copy-start.1 = (f32[1024]{0:T(1024)S(1)}, f32[1024]{0:T(1024)}, u32[]{:S(2)}) copy-start(f32[1024]{0:T(1024)} %param.11) | copy-start | bytes 12292

commit v4 on v3

--- a/solution.py
+++ b/solution.py
@@ -16,10 +16,16 @@
 bf16 = jnp.bfloat16
 VMEM = pltpu.VMEM
 MIB = 1 << 20
+EST = dict(side=6 * MIB, end=2 * MIB, left=MIB, corner=MIB, ends=MIB, own=MIB, sides=MIB, tail=MIB)
 
 
 def odd(axis):
     return lax.rem(lax.axis_index(axis), 2) == 1
+
+
+def at_end(axis):
+    index = lax.axis_index(axis)
+    return (index == 0) | (index == lax.axis_size(axis) - 1)
 
 
 def dot(a, b):
@@ -43,7 +49,7 @@
     return [slice(n * TILE, (n + 1) * TILE) for n in range(size // TILE)]
 
 
-def side_kernel(pattern, coupling, masked, c_near, c_far, raw, gates, sems, sem):
+def side_kernel(pattern, coupling, masked, e_near, e_far, raw, gates, sems, sem):
     rows, cols = masked.shape
     down, along = tiles_of(rows), tiles_of(cols)
     gate = pltpu.make_async_copy(pattern, gates, sem)
@@ -61,9 +67,25 @@
         for c, across in enumerate(along):
             tile = raw[part, across]
             masked[part, across] = jnp.where(gates[r, c] != 0, tile, jnp.zeros_like(tile))
-        first, last = masked[part, along[0]], masked[part, along[-1]]
-        c_near[part, :] = jnp.where(odd_t, first, last)
-        c_far[part, :] = jnp.where(odd_t, last, first)
+        if r in (0, len(down) - 1):
+            to = slice(0, H1) if r == 0 else slice(H1, 2 * H1)
+            first, last = masked[part, along[0]], masked[part, along[-1]]
+            e_near[to, :] = jnp.where(odd_t, first, last)
+            e_far[to, :] = jnp.where(odd_t, last, first)
+
+
+def end_kernel(masked, r_near, r_far):
+    rows, cols = masked.shape
+    first, last = masked[:H1, :], masked[rows - H1:, :]
+    odd_s = odd("src")
+    r_near[...] = jnp.where(odd_s, first, last)
+    r_far[...] = jnp.where(odd_s, last, first)
+
+
+def by_nearness(band, own, width, parity, out):
+    first, last = band[:, :width], band[:, own + width:]
+    out[:, :width] = jnp.where(parity, first, last)
+    out[:, width:] = jnp.where(parity, last, first)
 
 
 def band_copies(band, own, width, parity, out, sems):
@@ -79,67 +101,74 @@
     ]
 
 
-def end_kernel(masked, src_hbm, r_near, r_far, cost_src, sems):
+def left_kernel(masked, r_near, cost_src, tgt_hbm, m_near, m_far, left, src_ends, cost_tgt, sems):
     rows, cols = masked.shape
-    copies = band_copies(src_hbm, rows, H1, odd("src").astype(jnp.int32), cost_src, sems)
+    odd_t = odd("tgt")
+    copies = band_copies(tgt_hbm, cols, H2, odd_t.astype(jnp.int32), cost_tgt, sems)
     for copy in copies:
         copy.start()
-    first, last = masked[:H1, :], masked[rows - H1:, :]
-    odd_s = odd("src")
-    r_near[...] = jnp.where(odd_s, first, last)
-    r_far[...] = jnp.where(odd_s, last, first)
+    first, last = masked[H1:rows - H1, :H2], masked[H1:rows - H1, cols - H2:]
+    m_near[...] = jnp.where(odd_t, first, last)
+    m_far[...] = jnp.where(odd_t, last, first)
+    by_nearness(cost_src, rows, H1, odd("src"), src_ends)
+
+    @pl.when(at_end("src"))
+    def _():
+        src_ends[:, H1:] = jnp.zeros((rows, H1), bf16)
+
+    for across in tiles_of(cols):
+        bands = jnp.concatenate([cost_src[:, H1:H1 + rows], src_ends[:, :H1]], axis=1)
+        column = jnp.concatenate([masked[:, across], r_near[:, across]], axis=0)
+        left[:, across] = dot(bands, column)
     for copy in copies:
         copy.wait()
 
-
-def local_kernel(masked, cost_src, tgt_hbm, grad, cost_tgt, hi, lo, sems):
-    rows, cols = masked.shape
-    copies = band_copies(tgt_hbm, cols, H2, odd("tgt").astype(jnp.int32), cost_tgt, sems)
-    for copy in copies:
-        copy.start()
+    @pl.when(at_end("tgt"))
+    def _():
+        cost_tgt[:, cols + H2:] = jnp.zeros((cols, H2), bf16)
+
+
+def corner_kernel(e_near, e_far, _, x_near, x_far):
+    odd_s = odd("src")
+    for n, side in enumerate((e_near, e_far)):
+        across = slice(n * H2, (n + 1) * H2)
+        first, last = side[:H1, :], side[H1:, :]
+        x_near[:, across] = jnp.where(odd_s, first, last)
+        x_far[:, across] = jnp.where(odd_s, last, first)
+
+
+def ends_kernel(left, r_far, src_ends, hi, lo):
+    rows, cols = left.shape
     for across in tiles_of(cols):
-        hi[:, across], lo[:, across] = halves(dot(cost_src[:, :rows], masked[:, across]))
-    for copy in copies:
-        copy.wait()
+        value = left[:, across] + dot(src_ends[:, H1:], r_far[:, across])
+        hi[:, across], lo[:, across] = halves(value)
+
+
+def own_kernel(hi, lo, cost_tgt, grad):
+    rows, cols = grad.shape
+    both = jnp.concatenate([hi[...], lo[...]], axis=1)
     for across in tiles_of(cols):
         costs = cost_tgt[across, :cols]
-        both = jnp.concatenate([hi[...], lo[...]], axis=1)
         grad[:, across] = dot_t(both, jnp.concatenate([costs, costs], axis=1))
 
 
-def corner_kernel(c_near, c_far, x_near, x_far):
-    rows = c_near.shape[0]
-    odd_s = odd("src")
-    for n, side in enumerate((c_near, c_far)):
-        across = slice(n * H2, (n + 1) * H2)
-        first, last = side[:H1, :], side[rows - H1:, :]
-        x_near[:, across] = jnp.where(odd_s, first, last)
-        x_far[:, across] = jnp.where(odd_s, last, first)
-
-
-def halo_kernel(c_near, c_far, r_near, r_far, cost_src, cost_tgt, grad,
-                out, ends, hi, lo):
-    rows, cols = grad.shape
-    for n, side in enumerate((c_near, c_far)):
-        across = slice(n * H2, (n + 1) * H2)
-        hi[:, across], lo[:, across] = halves(dot(cost_src[:, :rows], side[...]))
-    for across in tiles_of(cols):
+def sides_kernel(e_near, e_far, m_near, m_far, cost_src, sides):
+    rows = cost_src.shape[0]
+    for n, (e, m) in enumerate(((e_near, m_near), (e_far, m_far))):
+        column = jnp.concatenate([e[:H1, :], m[...], e[H1:, :]], axis=0)
+        sides[:, n * H2:(n + 1) * H2] = dot(cost_src[:, H1:H1 + rows], column)
+
+
+def tail_kernel(x_near, x_far, sides, src_ends, cost_tgt, grad, masked,
+                kernel, totals, hi, lo, part):
+    rows, cols = masked.shape
+    for across in tiles_of(2 * H2):
+        corners = jnp.concatenate([x_near[:, across], x_far[:, across]], axis=0)
+        hi[:, across], lo[:, across] = halves(sides[:, across] + dot(src_ends[...], corners))
+    both = jnp.concatenate([hi[...], lo[...]], axis=1)
+    for n, across in enumerate(tiles_of(cols)):
         costs = cost_tgt[across, cols:]
-        both = jnp.concatenate([hi[...], lo[...]], axis=1)
-        out[:, across] = grad[:, across] + dot_t(both, jnp.concatenate([costs, costs], axis=1))
-    rim = jnp.concatenate([r_near[...], r_far[...]], axis=0)
-    for across in tiles_of(cols):
-        ends[:, across] = dot_t(rim, cost_tgt[across, :cols])
-
-
-def tail_kernel(x_near, x_far, cost_src, cost_tgt, ends, grad, masked, kernel, totals, part):
-    rows, cols = masked.shape
-    corners = jnp.concatenate([x_near[...], x_far[...]], axis=0)
-    bands = cost_src[:, rows:]
-    bands = jnp.concatenate([bands, bands], axis=1)
-    for n, across in enumerate(tiles_of(cols)):
-        hi, lo = halves(ends[:, across] + dot_t(corners, cost_tgt[across, cols:]))
-        slope = grad[:, across] + dot(bands, jnp.concatenate([hi, lo], axis=0))
+        slope = grad[:, across] + dot_t(both, jnp.concatenate([costs, costs], axis=1))
         value = masked[:, across].astype(f32) * jnp.exp(step_size * slope)
         kernel[:, across] = value
         sums = value[:, :LANES] + value[:, LANES:]
@@ -199,9 +228,7 @@
 
 def pair_plans(size):
     near = [(i, i ^ 1) for i in range(size)]
-    far = []
-    for i in range(1, size - 1, 2):
-        far += [(i, i + 1), (i + 1, i)]
+    far = [(i, (i + 1 if i % 2 else i - 1) % size) for i in range(size)]
     return near, far
 
 
@@ -216,10 +243,10 @@
     tiles = pattern.shape[0]
     dma = pltpu.SemaphoreType.DMA
 
-    masked, c_near, c_far = call(
+    masked, e_near, e_far = call(
         side_kernel,
         [pattern, coupling],
-        [((rows, cols), bf16)] + [((rows, H2), bf16)] * 2,
+        [((rows, cols), bf16)] + [((2 * H1, H2), bf16)] * 2,
         [
             VMEM((rows, cols), bf16),
             pltpu.SMEM(pattern.shape, pattern.dtype),
@@ -227,51 +254,54 @@
             dma,
         ],
         far=(0, 1),
-        moved=6 * MIB,
-    )
-    c_near, c_far = exchange(c_near, c_far, "tgt")
-    r_near, r_far, cost_src = call(
-        end_kernel,
-        [masked, cost_src],
-        [((H1, cols), bf16)] * 2 + [(cost_src.shape, bf16)],
+        moved=EST["side"],
+    )
+    e_near, e_far = exchange(e_near, e_far, "tgt")
+    r_near, r_far = call(
+        end_kernel, [masked], [((H1, cols), bf16)] * 2, [], moved=EST["end"]
+    )
+    r_near, r_far = exchange(r_near, r_far, "src")
+    m_near, m_far, left, src_ends, cost_tgt = call(
+        left_kernel,
+        [masked, r_near, cost_src, cost_tgt],
+        [((rows - 2 * H1, H2), bf16)] * 2
+        + [((rows, cols), f32), ((rows, 2 * H1), bf16), (cost_tgt.shape, bf16)],
         [dma((3,))],
-        far=(1,),
-        moved=5 * MIB,
-    )
-    r_near, r_far = exchange(r_near, r_far, "src")
-    grad, cost_tgt = call(
-        local_kernel,
-        [masked, cost_src, cost_tgt],
-        [((rows, cols), f32), (cost_tgt.shape, bf16)],
-        [VMEM((rows, cols), bf16)] * 2 + [dma((3,))],
-        far=(2,),
-        moved=MIB,
-    )
-
+        far=(3,),
+        moved=EST["left"],
+    )
+    m_near, m_far = exchange(m_near, m_far, "tgt")
     x_near, x_far = call(
         corner_kernel,
-        [c_near, c_far],
+        [e_near, e_far, src_ends],
         [((H1, 2 * H2), bf16)] * 2,
         [],
-        moved=1024 * MIB,
+        moved=EST["corner"],
     )
     x_near, x_far = exchange(x_near, x_far, "src")
-    grad, ends = call(
-        halo_kernel,
-        [c_near, c_far, r_near, r_far, cost_src, cost_tgt, grad],
-        [((rows, cols), f32), ((2 * H1, cols), f32)],
-        [VMEM((rows, 2 * H2), bf16)] * 2,
-        flops=2 * rows * cols * (2 * H1 + 6 * H2),
-        moved=10 * MIB,
+    hi, lo = call(
+        ends_kernel,
+        [left, r_far, src_ends],
+        [((rows, cols), bf16)] * 2,
+        [],
+        moved=EST["ends"],
+    )
+    grad = call(
+        own_kernel, [hi, lo, cost_tgt], [((rows, cols), f32)], [], moved=EST["own"]
+    )
+    sides = call(
+        sides_kernel,
+        [e_near, e_far, m_near, m_far, cost_src],
+        [((rows, 2 * H2), f32)],
+        [],
+        moved=EST["sides"],
     )
     kernel, totals = call(
         tail_kernel,
-        [x_near, x_far, cost_src, cost_tgt, ends, grad, masked],
+        [x_near, x_far, sides, src_ends, cost_tgt, grad, masked],
         [((rows, cols), f32), ((n_tgt, rows), f32)],
-        [VMEM((rows, LANES), f32)],
-        flops=2 * rows * cols * (4 * H1 + H2),
-        moved=16 * MIB,
-        exps=rows * cols,
+        [VMEM((rows, 2 * H2), bf16)] * 2 + [VMEM((rows, LANES), f32)],
+        moved=EST["tail"],
     )
     row_totals = lax.all_to_all(totals, "tgt", 0, 0, tiled=True)
     scaled, totals = call(

time: 67.2 us -> 61.2 us (0.911)
  Pallas kernels: 23.3 us -> 17.4 us
  starting transfers between devices: 11.2 us -> 16.6 us
  blocking collectives: 31.9 us -> 26.6 us
    pallas_call x8 -> x10, Pallas kernels: 23.3 us -> 17.4 us  [call(): pl.pallas_call(body, out_shape=shapes[0] if single else shapes, in_specs=...]
    ppermute x6 -> x8, starting transfers between devices: 11.2 us -> 16.6 us  [exchange(): return (lax.ppermute(first, axis, near), lax.ppermute(second, axis, far))]
    all_to_all x1, blocking collectives: 20.9 us -> 16 us  [per_device(): row_totals = lax.all_to_all(totals, 'tgt', 0, 0, tiled=True)]
  transfers between devices with their start and end apart: 6 -> 8, of which waited for: 0 -> 0; matrix products, arithmetic and copies ran while one was open for 0% -> 0% of each run, Pallas kernels for 22% -> 16%
where the time goes in v4:
time: 61.2 us; the launch traced here: 61 us
  blocking collectives  26.6 us (43%)
  Pallas kernels  17.4 us (28%)
  starting transfers between devices  16.6 us (27%)
    pallas_call x10, Pallas kernels, call(): pl.pallas_call(body, out_shape=shapes[0] if single else shapes, in_specs=...  17.4 us
    ppermute x8, starting transfers between devices, exchange(): return (lax.ppermute(first, axis, near), lax.ppermute(second, axis, far))  16.6 us
    all_to_all x1, blocking collectives, per_device(): row_totals = lax.all_to_all(totals, 'tgt', 0, 0, tiled=True)  16 us
    all_to_all x1, blocking collectives, per_device(): col_totals = lax.all_to_all(totals, 'src', 0, 0, tiled=True)  10.6 us
  transfers between devices with their start and end apart: 8, of which 0 were waited for; matrix products, arithmetic and copies ran while one was open for 0% of the time, Pallas kernels for 16%

profile of v4, /device:TPU:1, one launch (start us, length us, event | category | flops | bytes accessed | tf_op | source)
XLA Modules:
  0.0 61.0 jit_solution(4967536168247725152)
XLA Ops:
  0.0 1.8 %shard_map.64 = (bf16[1024,1024]{1,0:T(8,128)(2,1)S(1)}, bf16[512,256]{1,0:T(8,128)(2,1)S(1)}, bf16[512,256]{1,0:T(8,128)(2,1)S(1)}) custom-call(s32[4,4]{1,0:T(4,128)} %pattern.1, bf16[1024,1024]{1,0:T(8,128)(2,1)} %coupling.1), custom_call_target="tpu_custom_call" | custom-call | bytes 6291456 | tf_op jit(solution)/shard_map/pallas_call | solution.py:218
  1.8 0.1 shard_map.65
  1.9 3.3 %collective-permute-start.2 = (bf16[256,1024]{1,0:T(8,128)(2,1)S(1)}, bf16[256,1024]{1,0:T(8,128)(2,1)S(1)}, u32[]{:S(2)}, u32[]{:S(2)}) collective-permute-start(bf16[256,1024]{1,0:T(8,128)(2,1)S(1)} %get-tuple-element.26), channel_id=1, source_target_pairs={{0,32},{32,0},{64,96},{96,64},{128,160},{160,128},{192,224},{224,1... | collective-permute-start | bytes 1572872 | tf_op jit(solution)/shard_map/ppermute | solution.py:237
  5.2 0.0 collective-permute-start.7
  5.2 1.2 %collective-permute-start = (bf16[512,256]{1,0:T(8,128)(2,1)S(1)}, bf16[512,256]{1,0:T(8,128)(2,1)S(1)}, u32[]{:S(2)}, u32[]{:S(2)}) collective-permute-start(bf16[512,256]{1,0:T(8,128)(2,1)S(1)} %get-tuple-element.23), channel_id=1, source_target_pairs={{0,1},{1,0},{2,3},{3,2},{4,5},{5,4},{6,7},{7,6},{8,9},{9,8},{10,11... | collective-permute-start | bytes 786440 | tf_op jit(solution)/shard_map/ppermute | solution.py:237
  6.4 6.9 %collective-permute-start.1 = (bf16[512,256]{1,0:T(8,128)(2,1)S(1)}, bf16[512,256]{1,0:T(8,128)(2,1)S(1)}, u32[]{:S(2)}, u32[]{:S(2)}) collective-permute-start(bf16[512,256]{1,0:T(8,128)(2,1)S(1)} %get-tuple-element.24), channel_id=1, source_target_pairs={{0,31},{1,2},{2,1},{3,4},{4,3},{5,6},{6,5},{7,8},{8,7},{9,10},{10,... | collective-permute-start | bytes 786440 | tf_op jit(solution)/shard_map/ppermute | solution.py:237
  13.3 0.0 collective-permute-done.2.r_near
  13.3 3.1 %shard_map.66 = (bf16[512,256]{1,0:T(8,128)(2,1)S(1)}, bf16[512,256]{1,0:T(8,128)(2,1)S(1)}, f32[1024,1024]{1,0:T(8,128)S(1)}, bf16[1024,512]{1,0:T(8,128)(2,1)S(1)}, bf16[1024,1536]{1,0:T(8,128)(2,1)S(1)}) custom-call(bf16[1024,1024]{1,0:T(8,128)(2,1)S(1)} %get-tuple-element.25.masked, bf16[256,1024]{1,0:T(8,128)(2,1)S(1)} %collective-permute-done.2.r_near, ...), custom_call_target="tpu_custom_call" | custom-call | bytes 1048576 | tf_op jit(solution)/shard_map/pallas_call | solution.py:218
  16.4 0.1 collective-permute-start.5
  16.5 1.4 %collective-permute-start.6 = (bf16[512,256]{1,0:T(8,128)(2,1)S(1)}, bf16[512,256]{1,0:T(8,128)(2,1)S(1)}, u32[]{:S(2)}, u32[]{:S(2)}) collective-permute-start(bf16[512,256]{1,0:T(8,128)(2,1)S(1)} %get-tuple-element.31), channel_id=1, source_target_pairs={{0,31},{1,2},{2,1},{3,4},{4,3},{5,6},{6,5},{7,8},{8,7},{9,10},{10,... | collective-permute-start | bytes 786440 | tf_op jit(solution)/shard_map/ppermute | solution.py:237
  17.9 3.1 %collective-permute-start.3 = (bf16[256,512]{1,0:T(8,128)(2,1)S(1)}, bf16[256,512]{1,0:T(8,128)(2,1)S(1)}, u32[]{:S(2)}, u32[]{:S(2)}) collective-permute-start(bf16[256,512]{1,0:T(8,128)(2,1)S(1)} %get-tuple-element.28), channel_id=1, source_target_pairs={{0,32},{32,0},{64,96},{96,64},{128,160},{160,128},{192,224},{224,1... | collective-permute-start | bytes 786440 | tf_op jit(solution)/shard_map/ppermute | solution.py:237
  21.0 0.6 collective-permute-start.4
  21.6 0.0 collective-permute-done.7.r_far
  21.6 0.8 %shard_map.69 = (bf16[1024,1024]{1,0:T(8,128)(2,1)S(1)}, bf16[1024,1024]{1,0:T(8,128)(2,1)S(1)}) custom-call(f32[1024,1024]{1,0:T(8,128)S(1)} %get-tuple-element.33.left, bf16[256,1024]{1,0:T(8,128)(2,1)S(1)} %collective-permute-done.7.r_far, bf16[1024,512]{1,0:T(8,128)(2,1)S(1)} %get-tuple-element.27._.src_ends), custom_call_target="tpu_custom_call" | custom-call | bytes 1048576 | tf_op jit(solution)/shard_map/pallas_call | solution.py:218
  22.5 4.5 %shard_map.70.grad = f32[1024,1024]{1,0:T(8,128)S(1)} custom-call(bf16[1024,1024]{1,0:T(8,128)(2,1)S(1)} %get-tuple-element.35.hi, bf16[1024,1024]{1,0:T(8,128)(2,1)S(1)} %get-tuple-element.36.lo, bf16[1024,1536]{1,0:T(8,128)(2,1)S(1)} %get-tuple-element.32.cost_tgt), custom_call_target="tpu_custom_call" | custom-call | bytes 1048576 | tf_op jit(solution)/shard_map/pallas_call | solution.py:218
  27.0 1.2 %shard_map.68.sides = f32[1024,512]{1,0:T(8,128)S(1)} custom-call(bf16[512,256]{1,0:T(8,128)(2,1)S(1)} %collective-permute-done.e_near, bf16[512,256]{1,0:T(8,128)(2,1)S(1)} %collective-permute-done.1.e_far, bf16[512,256]{1,0:T(8,128)(2,1)S(1)} %collective-permute-done.5.m_near, bf16[512,256]{1,0:T(8,128)(2,1)S(1)} %collective-permute-done.6.m_far, ...), custom_call_target="tpu_custom_call" | custom-call | bytes 1048576 | tf_op jit(solution)/shard_map/pallas_call | solution.py:218
  28.3 0.0 copy-start.1
  28.3 3.2 %shard_map.71 = (f32[1024,1024]{1,0:T(8,128)S(1)}, f32[32,1024]{1,0:T(8,128)S(1)}) custom-call(bf16[256,512]{1,0:T(8,128)(2,1)S(1)} %collective-permute-done.3.x_near, bf16[256,512]{1,0:T(8,128)(2,1)S(1)} %collective-permute-done.4.x_far, f32[1024,512]{1,0:T(8,128)S(1)} %shard_map.68.sides, bf16[1024,512]{1,0:T(8,128)(2,1)S(1)} %get-tuple-element.27._.src_ends, ...), custom_call_target="tpu_custom_call" | custom-call | bytes 1048576 | tf_op jit(solution)/shard_map/pallas_call | solution.py:218
  31.5 0.0 copy-start.2
  31.5 0.1 copy.7
  31.6 16.0 %all_to_all.22 = f32[32,1,1024]{2,1,0:T(1,128)S(1)} all-to-all(f32[32,1,1024]{2,1,0:T(1,128)S(1)} %copy.7), channel_id=1, replica_groups=mesh['src'=8,'tgt'=32] {'tgt'}, dimensions={0} | all-to-all | bytes 262144 | tf_op jit(solution)/shard_map/all_to_all | solution.py:306
  47.6 0.5 shard_map.72
  48.1 10.6 %all_to_all.23 = f32[8,1,1024]{2,1,0:T(1,128)S(1)} all-to-all(f32[8,1,1024]{2,1,0:T(1,128)S(1)} %copy.8), channel_id=1, replica_groups=mesh['src'=8,'tgt'=32] {'src'}, dimensions={0} | all-to-all | bytes 65536 | tf_op jit(solution)/shard_map/all_to_all | solution.py:314
  58.8 2.1 %shard_map.73 = f32[1024,1024]{1,0:T(8,128)} custom-call(f32[8,1024]{1,0:T(8,128)S(1)} %bitcast.11, f32[1,1024]{1,0:T(1,128)S(1)} %bitcast.15, f32[1024,1024]{1,0:T(8,128)S(1)} %get-tuple-element.40.refs_2_), custom_call_target="tpu_custom_call" | custom-call | bytes 8388608 | tf_op jit(solution)/shard_map/pallas_call | solution.py:218
  (14 shorter events, 0.1 us)
Async XLA Ops:
  0.0 13.3 %copy-start = (bf16[1024,1536]{1,0:T(8,128)(2,1)S(1)}, bf16[1024,1536]{1,0:T(8,128)(2,1)}, u32[]{:S(2)}) copy-start(bf16[1024,1536]{1,0:T(8,128)(2,1)} %cost_src.3) | copy-start | bytes 9437188
  1.9 11.4 %collective-permute-start.2 = (bf16[256,1024]{1,0:T(8,128)(2,1)S(1)}, bf16[256,1024]{1,0:T(8,128)(2,1)S(1)}, u32[]{:S(2)}, u32[]{:S(2)}) collective-permute-start(bf16[256,1024]{1,0:T(8,128)(2,1)S(1)} %get-tuple-element.26), channel_id=1, source_target_pairs={{0,32},{32,0},{64,96},{96,64},{128,160},{160,128},{192,224},{224,1... | collective-permute-start | bytes 1572872 | tf_op jit(solution)/shard_map/ppermute | solution.py:237
  5.2 16.4 %collective-permute-start.7 = (bf16[256,1024]{1,0:T(8,128)(2,1)S(1)}, bf16[256,1024]{1,0:T(8,128)(2,1)S(1)}, u32[]{:S(2)}, u32[]{:S(2)}) collective-permute-start(bf16[256,1024]{1,0:T(8,128)(2,1)S(1)} %get-tuple-element.34), channel_id=1, source_target_pairs={{0,224},{32,64},{64,32},{96,128},{128,96},{160,192},{192,160},{224... | collective-permute-start | bytes 1572872 | tf_op jit(solution)/shard_map/ppermute | solution.py:237
  5.2 12.6 %collective-permute-start = (bf16[512,256]{1,0:T(8,128)(2,1)S(1)}, bf16[512,256]{1,0:T(8,128)(2,1)S(1)}, u32[]{:S(2)}, u32[]{:S(2)}) collective-permute-start(bf16[512,256]{1,0:T(8,128)(2,1)S(1)} %get-tuple-element.23), channel_id=1, source_target_pairs={{0,1},{1,0},{2,3},{3,2},{4,5},{5,4},{6,7},{7,6},{8,9},{9,8},{10,11... | collective-permute-start | bytes 786440 | tf_op jit(solution)/shard_map/ppermute | solution.py:237
  6.4 11.5 %collective-permute-start.1 = (bf16[512,256]{1,0:T(8,128)(2,1)S(1)}, bf16[512,256]{1,0:T(8,128)(2,1)S(1)}, u32[]{:S(2)}, u32[]{:S(2)}) collective-permute-start(bf16[512,256]{1,0:T(8,128)(2,1)S(1)} %get-tuple-element.24), channel_id=1, source_target_pairs={{0,31},{1,2},{2,1},{3,4},{4,3},{5,6},{6,5},{7,8},{8,7},{9,10},{10,... | collective-permute-start | bytes 786440 | tf_op jit(solution)/shard_map/ppermute | solution.py:237
  16.4 10.6 %collective-permute-start.5 = (bf16[512,256]{1,0:T(8,128)(2,1)S(1)}, bf16[512,256]{1,0:T(8,128)(2,1)S(1)}, u32[]{:S(2)}, u32[]{:S(2)}) collective-permute-start(bf16[512,256]{1,0:T(8,128)(2,1)S(1)} %get-tuple-element.30), channel_id=1, source_target_pairs={{0,1},{1,0},{2,3},{3,2},{4,5},{5,4},{6,7},{7,6},{8,9},{9,8},{10,11... | collective-permute-start | bytes 786440 | tf_op jit(solution)/shard_map/ppermute | solution.py:237
  16.5 10.6 %collective-permute-start.6 = (bf16[512,256]{1,0:T(8,128)(2,1)S(1)}, bf16[512,256]{1,0:T(8,128)(2,1)S(1)}, u32[]{:S(2)}, u32[]{:S(2)}) collective-permute-start(bf16[512,256]{1,0:T(8,128)(2,1)S(1)} %get-tuple-element.31), channel_id=1, source_target_pairs={{0,31},{1,2},{2,1},{3,4},{4,3},{5,6},{6,5},{7,8},{8,7},{9,10},{10,... | collective-permute-start | bytes 786440 | tf_op jit(solution)/shard_map/ppermute | solution.py:237
  17.9 10.4 %collective-permute-start.3 = (bf16[256,512]{1,0:T(8,128)(2,1)S(1)}, bf16[256,512]{1,0:T(8,128)(2,1)S(1)}, u32[]{:S(2)}, u32[]{:S(2)}) collective-permute-start(bf16[256,512]{1,0:T(8,128)(2,1)S(1)} %get-tuple-element.28), channel_id=1, source_target_pairs={{0,32},{32,0},{64,96},{96,64},{128,160},{160,128},{192,224},{224,1... | collective-permute-start | bytes 786440 | tf_op jit(solution)/shard_map/ppermute | solution.py:237
  21.0 7.3 %collective-permute-start.4 = (bf16[256,512]{1,0:T(8,128)(2,1)S(1)}, bf16[256,512]{1,0:T(8,128)(2,1)S(1)}, u32[]{:S(2)}, u32[]{:S(2)}) collective-permute-start(bf16[256,512]{1,0:T(8,128)(2,1)S(1)} %get-tuple-element.29), channel_id=1, source_target_pairs={{0,224},{32,64},{64,32},{96,128},{128,96},{160,192},{192,160},{224... | collective-permute-start | bytes 786440 | tf_op jit(solution)/shard_map/ppermute | solution.py:237
  28.3 19.3 %copy-start.1 = (f32[1024]{0:T(1024)S(1)}, f32[1024]{0:T(1024)}, u32[]{:S(2)}) copy-start(f32[1024]{0:T(1024)} %param.10) | copy-start | bytes 12292
  31.5 27.3 %copy-start.2 = (f32[1024]{0:T(1024)S(1)}, f32[1024]{0:T(1024)}, u32[]{:S(2)}) copy-start(f32[1024]{0:T(1024)} %param.11) | copy-start | bytes 12292

commit v5 on v4

--- a/solution.py
+++ b/solution.py
@@ -13,6 +13,8 @@
 step_size = 1.0
 
 f32 = jnp.float32
+f8 = jnp.float8_e4m3fn
+SCALE = 512.0
 bf16 = jnp.bfloat16
 VMEM = pltpu.VMEM
 MIB = 1 << 20
@@ -38,7 +40,11 @@
 
 def halves(x):
     hi = x.astype(bf16)
-    return hi, (x - hi.astype(f32)).astype(bf16)
+    return hi, ((x - hi.astype(f32)) * SCALE).astype(f8)
+
+
+def two_dots(hi, lo, costs, small):
+    return dot_t(hi, costs) + dot_t(lo, small) * (1 / SCALE**2)
 
 
 def as_row(x):
@@ -101,7 +107,8 @@
     ]
 
 
-def left_kernel(masked, r_near, cost_src, tgt_hbm, m_near, m_far, left, src_ends, cost_tgt, sems):
+def left_kernel(masked, r_near, cost_src, tgt_hbm,
+                m_near, m_far, left, src_ends, cost_tgt, sems):
     rows, cols = masked.shape
     odd_t = odd("tgt")
     copies = band_copies(tgt_hbm, cols, H2, odd_t.astype(jnp.int32), cost_tgt, sems)
@@ -137,19 +144,20 @@
         x_far[:, across] = jnp.where(odd_s, last, first)
 
 
-def ends_kernel(left, r_far, src_ends, hi, lo):
+def ends_kernel(left, r_far, src_ends, cost_tgt, hi, lo, small_tgt):
     rows, cols = left.shape
+    small_tgt[...] = (cost_tgt[...].astype(f32) * SCALE).astype(f8)
     for across in tiles_of(cols):
         value = left[:, across] + dot(src_ends[:, H1:], r_far[:, across])
         hi[:, across], lo[:, across] = halves(value)
 
 
-def own_kernel(hi, lo, cost_tgt, grad):
+def own_kernel(hi, lo, cost_tgt, small_tgt, grad):
     rows, cols = grad.shape
-    both = jnp.concatenate([hi[...], lo[...]], axis=1)
     for across in tiles_of(cols):
-        costs = cost_tgt[across, :cols]
-        grad[:, across] = dot_t(both, jnp.concatenate([costs, costs], axis=1))
+        grad[:, across] = two_dots(
+            hi[...], lo[...], cost_tgt[across, :cols], small_tgt[across, :cols]
+        )
 
 
 def sides_kernel(e_near, e_far, m_near, m_far, cost_src, sides):
@@ -159,38 +167,38 @@
         sides[:, n * H2:(n + 1) * H2] = dot(cost_src[:, H1:H1 + rows], column)
 
 
-def tail_kernel(x_near, x_far, sides, src_ends, cost_tgt, grad, masked,
+def tail_kernel(x_near, x_far, sides, src_ends, cost_tgt, small_tgt, grad, masked,
                 kernel, totals, hi, lo, part):
     rows, cols = masked.shape
     for across in tiles_of(2 * H2):
         corners = jnp.concatenate([x_near[:, across], x_far[:, across]], axis=0)
         hi[:, across], lo[:, across] = halves(sides[:, across] + dot(src_ends[...], corners))
-    both = jnp.concatenate([hi[...], lo[...]], axis=1)
     for n, across in enumerate(tiles_of(cols)):
-        costs = cost_tgt[across, cols:]
-        slope = grad[:, across] + dot_t(both, jnp.concatenate([costs, costs], axis=1))
+        slope = grad[:, across] + two_dots(
+            hi[...], lo[...], cost_tgt[across, cols:], small_tgt[across, cols:]
+        )
         value = masked[:, across].astype(f32) * jnp.exp(step_size * slope)
         kernel[:, across] = value
         sums = value[:, :LANES] + value[:, LANES:]
         part[...] = sums if n == 0 else part[...] + sums
-    totals[...] = jnp.broadcast_to(as_row(part[...]), totals.shape)
+    totals[...] = jnp.broadcast_to(as_row(part[...])[None], totals.shape)
 
 
 def column_kernel(total, row_totals, mass, kernel, scaled, totals):
     rows, cols = kernel.shape
-    factor = mass[...] * total / jnp.sum(row_totals[...], axis=0, keepdims=True)
+    factor = mass[...] * total / jnp.sum(row_totals[...], axis=0)
     factor = jnp.broadcast_to(factor, (LANES, rows)).T
     for n in range(cols // LANES):
         across = slice(n * LANES, (n + 1) * LANES)
         value = kernel[:, across] * factor
         scaled[:, across] = value
         sums = jnp.sum(value, axis=0, keepdims=True)
-        totals[:, across] = jnp.broadcast_to(sums, (totals.shape[0], LANES))
+        totals[:, :, across] = jnp.broadcast_to(sums[None], (totals.shape[0], 1, LANES))
 
 
 def last_kernel(total, col_totals, mass, scaled, out, block, sems):
     rows, cols = scaled.shape
-    factor = mass[...] * total / jnp.sum(col_totals[...], axis=0, keepdims=True)
+    factor = mass[...] * total / jnp.sum(col_totals[...], axis=0)
     n_blocks = sems.shape[0]
     size = rows // n_blocks
 
@@ -271,23 +279,23 @@
         moved=EST["left"],
     )
     m_near, m_far = exchange(m_near, m_far, "tgt")
+    hi, lo, small_tgt = call(
+        ends_kernel,
+        [left, r_far, src_ends, cost_tgt],
+        [((rows, cols), bf16), ((rows, cols), f8), (cost_tgt.shape, f8)],
+        [],
+        moved=EST["ends"],
+    )
     x_near, x_far = call(
         corner_kernel,
-        [e_near, e_far, src_ends],
+        [e_near, e_far, lo],
         [((H1, 2 * H2), bf16)] * 2,
         [],
         moved=EST["corner"],
     )
     x_near, x_far = exchange(x_near, x_far, "src")
-    hi, lo = call(
-        ends_kernel,
-        [left, r_far, src_ends],
-        [((rows, cols), bf16)] * 2,
-        [],
-        moved=EST["ends"],
-    )
     grad = call(
-        own_kernel, [hi, lo, cost_tgt], [((rows, cols), f32)], [], moved=EST["own"]
+        own_kernel, [hi, lo, cost_tgt, small_tgt], [((rows, cols), f32)], [], moved=EST["own"]
     )
     sides = call(
         sides_kernel,
@@ -298,16 +306,16 @@
     )
     kernel, totals = call(
         tail_kernel,
-        [x_near, x_far, sides, src_ends, cost_tgt, grad, masked],
-        [((rows, cols), f32), ((n_tgt, rows), f32)],
-        [VMEM((rows, 2 * H2), bf16)] * 2 + [VMEM((rows, LANES), f32)],
+        [x_near, x_far, sides, src_ends, cost_tgt, small_tgt, grad, masked],
+        [((rows, cols), f32), ((n_tgt, 1, rows), f32)],
+        [VMEM((rows, 2 * H2), bf16), VMEM((rows, 2 * H2), f8), VMEM((rows, LANES), f32)],
         moved=EST["tail"],
     )
     row_totals = lax.all_to_all(totals, "tgt", 0, 0, tiled=True)
     scaled, totals = call(
         lambda *refs: column_kernel(float(cols * n_tgt), *refs),
         [row_totals, mass_src[None, :], kernel],
-        [((rows, cols), f32), ((n_src, cols), f32)],
+        [((rows, cols), f32), ((n_src, 1, cols), f32)],
         [],
         moved=8 * MIB,
     )

time: 61.2 us -> 58.9 us (0.962)
  blocking collectives: 26.6 us -> 23.8 us
  waiting for transfers between devices: 0.02 us -> 1.37 us
    all_to_all x1, blocking collectives: 16 us -> 14 us  [per_device(): row_totals = lax.all_to_all(totals, 'tgt', 0, 0, tiled=True)]
    ppermute x8, waiting for transfers between devices: 0.02 us -> 1.37 us  [exchange(): return (lax.ppermute(first, axis, near), lax.ppermute(second, axis, far))]
    all_to_all x1, blocking collectives: 10.6 us -> 9.8 us  [per_device(): col_totals = lax.all_to_all(totals, 'src', 0, 0, tiled=True)]
  transfers between devices with their start and end apart: 8 -> 8, of which waited for: 0 -> 1; matrix products, arithmetic and copies ran while one was open for 0% -> 0% of each run, Pallas kernels for 16% -> 17%
where the time goes in v5:
time: 58.9 us; the launch traced here: 58.7 us
  blocking collectives  23.8 us (40%)
  Pallas kernels  17.3 us (29%)
  starting transfers between devices  16 us (27%)
  waiting for transfers between devices  1.37 us (2%)
    pallas_call x10, Pallas kernels, call(): pl.pallas_call(body, out_shape=shapes[0] if single else shapes, in_specs=...  17.3 us
    ppermute x8, starting transfers between devices, exchange(): return (lax.ppermute(first, axis, near), lax.ppermute(second, axis, far))  16 us
    all_to_all x1, blocking collectives, per_device(): row_totals = lax.all_to_all(totals, 'tgt', 0, 0, tiled=True)  14 us
    all_to_all x1, blocking collectives, per_device(): col_totals = lax.all_to_all(totals, 'src', 0, 0, tiled=True)  9.8 us
    ppermute x8, waiting for transfers between devices, exchange(): return (lax.ppermute(first, axis, near), lax.ppermute(second, axis, far))  1.37 us
  transfers between devices with their start and end apart: 8, of which 1 were waited for; matrix products, arithmetic and copies ran while one was open for 0% of the time, Pallas kernels for 17%

profile of v5, /device:TPU:1, one launch (start us, length us, event | category | flops | bytes accessed | tf_op | source)
XLA Modules:
  0.0 58.7 jit_solution(12549297751918951198)
XLA Ops:
  0.0 1.8 %shard_map.64 = (bf16[1024,1024]{1,0:T(8,128)(2,1)S(1)}, bf16[512,256]{1,0:T(8,128)(2,1)S(1)}, bf16[512,256]{1,0:T(8,128)(2,1)S(1)}) custom-call(s32[4,4]{1,0:T(4,128)} %pattern.1, bf16[1024,1024]{1,0:T(8,128)(2,1)} %coupling.1), custom_call_target="tpu_custom_call" | custom-call | bytes 6291456 | tf_op jit(solution)/shard_map/pallas_call | solution.py:226
  1.8 0.1 shard_map.65
  1.9 3.3 %collective-permute-start.2 = (bf16[256,1024]{1,0:T(8,128)(2,1)S(1)}, bf16[256,1024]{1,0:T(8,128)(2,1)S(1)}, u32[]{:S(2)}, u32[]{:S(2)}) collective-permute-start(bf16[256,1024]{1,0:T(8,128)(2,1)S(1)} %get-tuple-element.27), channel_id=1, source_target_pairs={{0,32},{32,0},{64,96},{96,64},{128,160},{160,128},{192,224},{224,1... | collective-permute-start | bytes 1572872 | tf_op jit(solution)/shard_map/ppermute | solution.py:245
  5.2 0.0 collective-permute-start.3
  5.2 1.2 %collective-permute-start = (bf16[512,256]{1,0:T(8,128)(2,1)S(1)}, bf16[512,256]{1,0:T(8,128)(2,1)S(1)}, u32[]{:S(2)}, u32[]{:S(2)}) collective-permute-start(bf16[512,256]{1,0:T(8,128)(2,1)S(1)} %get-tuple-element.24), channel_id=1, source_target_pairs={{0,1},{1,0},{2,3},{3,2},{4,5},{5,4},{6,7},{7,6},{8,9},{9,8},{10,11... | collective-permute-start | bytes 786440 | tf_op jit(solution)/shard_map/ppermute | solution.py:245
  6.4 6.9 %collective-permute-start.1 = (bf16[512,256]{1,0:T(8,128)(2,1)S(1)}, bf16[512,256]{1,0:T(8,128)(2,1)S(1)}, u32[]{:S(2)}, u32[]{:S(2)}) collective-permute-start(bf16[512,256]{1,0:T(8,128)(2,1)S(1)} %get-tuple-element.25), channel_id=1, source_target_pairs={{0,31},{1,2},{2,1},{3,4},{4,3},{5,6},{6,5},{7,8},{8,7},{9,10},{10,... | collective-permute-start | bytes 786440 | tf_op jit(solution)/shard_map/ppermute | solution.py:245
  13.3 0.0 collective-permute-done.2.r_near
  13.3 3.1 %shard_map.66 = (bf16[512,256]{1,0:T(8,128)(2,1)S(1)}, bf16[512,256]{1,0:T(8,128)(2,1)S(1)}, f32[1024,1024]{1,0:T(8,128)S(1)}, bf16[1024,512]{1,0:T(8,128)(2,1)S(1)}, bf16[1024,1536]{1,0:T(8,128)(2,1)S(1)}) custom-call(bf16[1024,1024]{1,0:T(8,128)(2,1)S(1)} %get-tuple-element.26.masked, bf16[256,1024]{1,0:T(8,128)(2,1)S(1)} %collective-permute-done.2.r_near, ...), custom_call_target="tpu_custom_call" | custom-call | bytes 1048576 | tf_op jit(solution)/shard_map/pallas_call | solution.py:226
  16.4 0.1 collective-permute-start.6
  16.5 1.4 %collective-permute-start.7 = (bf16[512,256]{1,0:T(8,128)(2,1)S(1)}, bf16[512,256]{1,0:T(8,128)(2,1)S(1)}, u32[]{:S(2)}, u32[]{:S(2)}) collective-permute-start(bf16[512,256]{1,0:T(8,128)(2,1)S(1)} %get-tuple-element.36), channel_id=1, source_target_pairs={{0,31},{1,2},{2,1},{3,4},{4,3},{5,6},{6,5},{7,8},{8,7},{9,10},{10,... | collective-permute-start | bytes 786440 | tf_op jit(solution)/shard_map/ppermute | solution.py:245
  17.9 2.0 %shard_map.67 = (bf16[1024,1024]{1,0:T(8,128)(2,1)S(1)}, f8e4m3fn[1024,1024]{1,0:T(32,128)(4,1)S(1)}, f8e4m3fn[1024,1536]{1,0:T(32,128)(4,1)S(1)}) custom-call(f32[1024,1024]{1,0:T(8,128)S(1)} %get-tuple-element.28.left, bf16[256,1024]{1,0:T(8,128)(2,1)S(1)} %collective-permute-done.3.r_far, bf16[1024,512]{1,0:T(8,128)(2,1)S(1)} %get-tuple-element.30.src_ends, ...), custom_call_target="tpu_custom_call" | custom-call | bytes 1048576 | tf_op jit(solution)/shard_map/pallas_call | solution.py:226
  19.9 0.1 shard_map.68
  19.9 3.1 %collective-permute-start.4 = (bf16[256,512]{1,0:T(8,128)(2,1)S(1)}, bf16[256,512]{1,0:T(8,128)(2,1)S(1)}, u32[]{:S(2)}, u32[]{:S(2)}) collective-permute-start(bf16[256,512]{1,0:T(8,128)(2,1)S(1)} %get-tuple-element.33), channel_id=1, source_target_pairs={{0,32},{32,0},{64,96},{96,64},{128,160},{160,128},{192,224},{224,1... | collective-permute-start | bytes 786440 | tf_op jit(solution)/shard_map/ppermute | solution.py:245
  23.0 0.0 collective-permute-start.5
  23.0 3.4 %shard_map.70.grad = f32[1024,1024]{1,0:T(8,128)S(1)} custom-call(bf16[1024,1024]{1,0:T(8,128)(2,1)S(1)} %get-tuple-element.38.hi, f8e4m3fn[1024,1024]{1,0:T(32,128)(4,1)S(1)} %get-tuple-element.32._.lo, bf16[1024,1536]{1,0:T(8,128)(2,1)S(1)} %get-tuple-element.31.cost_tgt, f8e4m3fn[1024,1536]{1,0:T(32,128)(4,1)S(1)} %get-tuple-element.37.small_tgt), custom_call_target="tpu_custom_call" | custom-call | bytes 1048576 | tf_op jit(solution)/shard_map/pallas_call | solution.py:226
  26.5 1.2 %shard_map.69.sides = f32[1024,512]{1,0:T(8,128)S(1)} custom-call(bf16[512,256]{1,0:T(8,128)(2,1)S(1)} %collective-permute-done.e_near, bf16[512,256]{1,0:T(8,128)(2,1)S(1)} %collective-permute-done.1.e_far, bf16[512,256]{1,0:T(8,128)(2,1)S(1)} %collective-permute-done.6.m_near, bf16[512,256]{1,0:T(8,128)(2,1)S(1)} %collective-permute-done.7.m_far, ...), custom_call_target="tpu_custom_call" | custom-call | bytes 1048576 | tf_op jit(solution)/shard_map/pallas_call | solution.py:226
  27.7 0.0 copy-start.1
  27.8 1.4 %collective-permute-done.5.x_far = bf16[256,512]{1,0:T(8,128)(2,1)S(1)} collective-permute-done((bf16[256,512]{1,0:T(8,128)(2,1)S(1)}, bf16[256,512]{1,0:T(8,128)(2,1)S(1)}, u32[]{:S(2)}, u32[]{:S(2)}) %collective-permute-start.5) | collective-permute-done | bytes 262176 | tf_op jit(solution)/shard_map/ppermute | solution.py:245
  29.1 2.9 %shard_map.71 = (f32[1024,1024]{1,0:T(8,128)S(1)}, f32[32,1,1024]{2,1,0:T(1,128)S(1)}) custom-call(bf16[256,512]{1,0:T(8,128)(2,1)S(1)} %collective-permute-done.4.x_near, bf16[256,512]{1,0:T(8,128)(2,1)S(1)} %collective-permute-done.5.x_far, f32[1024,512]{1,0:T(8,128)S(1)} %shard_map.69.sides, bf16[1024,512]{1,0:T(8,128)(2,1)S(1)} %get-tuple-element.30.src_ends, ...), custom_call_target="tpu_custom_call" | custom-call | bytes 1048576 | tf_op jit(solution)/shard_map/pallas_call | solution.py:226
  32.1 0.0 copy-start.2
  32.1 14.0 %all_to_all.10.refs_0_ = f32[32,1,1024]{2,1,0:T(1,128)S(1)} all-to-all(f32[32,1,1024]{2,1,0:T(1,128)S(1)} %get-tuple-element.39), channel_id=1, replica_groups=mesh['src'=8,'tgt'=32] {'tgt'}, dimensions={0} | all-to-all | bytes 262144 | tf_op jit(solution)/shard_map/all_to_all | solution.py:314
  46.1 0.5 shard_map.72
  46.6 9.8 %all_to_all.11.refs_0_ = f32[8,1,1024]{2,1,0:T(1,128)S(1)} all-to-all(f32[8,1,1024]{2,1,0:T(1,128)S(1)} %get-tuple-element.41), channel_id=1, replica_groups=mesh['src'=8,'tgt'=32] {'src'}, dimensions={0} | all-to-all | bytes 65536 | tf_op jit(solution)/shard_map/all_to_all | solution.py:322
  56.4 2.1 %shard_map.73 = f32[1024,1024]{1,0:T(8,128)} custom-call(f32[8,1,1024]{2,1,0:T(1,128)S(1)} %all_to_all.11.refs_0_, f32[1,1024]{1,0:T(1,128)S(1)} %bitcast.3, f32[1024,1024]{1,0:T(8,128)S(1)} %get-tuple-element.42.refs_2_), custom_call_target="tpu_custom_call" | custom-call | bytes 8388608 | tf_op jit(solution)/shard_map/pallas_call | solution.py:226
  (10 shorter events, 0.0 us)
Async XLA Ops:
  0.0 13.3 %copy-start = (bf16[1024,1536]{1,0:T(8,128)(2,1)S(1)}, bf16[1024,1536]{1,0:T(8,128)(2,1)}, u32[]{:S(2)}) copy-start(bf16[1024,1536]{1,0:T(8,128)(2,1)} %cost_src.3) | copy-start | bytes 9437188
  1.9 11.4 %collective-permute-start.2 = (bf16[256,1024]{1,0:T(8,128)(2,1)S(1)}, bf16[256,1024]{1,0:T(8,128)(2,1)S(1)}, u32[]{:S(2)}, u32[]{:S(2)}) collective-permute-start(bf16[256,1024]{1,0:T(8,128)(2,1)S(1)} %get-tuple-element.27), channel_id=1, source_target_pairs={{0,32},{32,0},{64,96},{96,64},{128,160},{160,128},{192,224},{224,1... | collective-permute-start | bytes 1572872 | tf_op jit(solution)/shard_map/ppermute | solution.py:245
  5.2 12.6 %collective-permute-start.3 = (bf16[256,1024]{1,0:T(8,128)(2,1)S(1)}, bf16[256,1024]{1,0:T(8,128)(2,1)S(1)}, u32[]{:S(2)}, u32[]{:S(2)}) collective-permute-start(bf16[256,1024]{1,0:T(8,128)(2,1)S(1)} %get-tuple-element.29), channel_id=1, source_target_pairs={{0,224},{32,64},{64,32},{96,128},{128,96},{160,192},{192,160},{224... | collective-permute-start | bytes 1572872 | tf_op jit(solution)/shard_map/ppermute | solution.py:245
  5.2 14.6 %collective-permute-start = (bf16[512,256]{1,0:T(8,128)(2,1)S(1)}, bf16[512,256]{1,0:T(8,128)(2,1)S(1)}, u32[]{:S(2)}, u32[]{:S(2)}) collective-permute-start(bf16[512,256]{1,0:T(8,128)(2,1)S(1)} %get-tuple-element.24), channel_id=1, source_target_pairs={{0,1},{1,0},{2,3},{3,2},{4,5},{5,4},{6,7},{7,6},{8,9},{9,8},{10,11... | collective-permute-start | bytes 786440 | tf_op jit(solution)/shard_map/ppermute | solution.py:245
  6.4 13.5 %collective-permute-start.1 = (bf16[512,256]{1,0:T(8,128)(2,1)S(1)}, bf16[512,256]{1,0:T(8,128)(2,1)S(1)}, u32[]{:S(2)}, u32[]{:S(2)}) collective-permute-start(bf16[512,256]{1,0:T(8,128)(2,1)S(1)} %get-tuple-element.25), channel_id=1, source_target_pairs={{0,31},{1,2},{2,1},{3,4},{4,3},{5,6},{6,5},{7,8},{8,7},{9,10},{10,... | collective-permute-start | bytes 786440 | tf_op jit(solution)/shard_map/ppermute | solution.py:245
  16.4 10.1 %collective-permute-start.6 = (bf16[512,256]{1,0:T(8,128)(2,1)S(1)}, bf16[512,256]{1,0:T(8,128)(2,1)S(1)}, u32[]{:S(2)}, u32[]{:S(2)}) collective-permute-start(bf16[512,256]{1,0:T(8,128)(2,1)S(1)} %get-tuple-element.35), channel_id=1, source_target_pairs={{0,1},{1,0},{2,3},{3,2},{4,5},{5,4},{6,7},{7,6},{8,9},{9,8},{10,11... | collective-permute-start | bytes 786440 | tf_op jit(solution)/shard_map/ppermute | solution.py:245
  16.5 10.0 %collective-permute-start.7 = (bf16[512,256]{1,0:T(8,128)(2,1)S(1)}, bf16[512,256]{1,0:T(8,128)(2,1)S(1)}, u32[]{:S(2)}, u32[]{:S(2)}) collective-permute-start(bf16[512,256]{1,0:T(8,128)(2,1)S(1)} %get-tuple-element.36), channel_id=1, source_target_pairs={{0,31},{1,2},{2,1},{3,4},{4,3},{5,6},{6,5},{7,8},{8,7},{9,10},{10,... | collective-permute-start | bytes 786440 | tf_op jit(solution)/shard_map/ppermute | solution.py:245
  19.9 7.8 %collective-permute-start.4 = (bf16[256,512]{1,0:T(8,128)(2,1)S(1)}, bf16[256,512]{1,0:T(8,128)(2,1)S(1)}, u32[]{:S(2)}, u32[]{:S(2)}) collective-permute-start(bf16[256,512]{1,0:T(8,128)(2,1)S(1)} %get-tuple-element.33), channel_id=1, source_target_pairs={{0,32},{32,0},{64,96},{96,64},{128,160},{160,128},{192,224},{224,1... | collective-permute-start | bytes 786440 | tf_op jit(solution)/shard_map/ppermute | solution.py:245
  23.0 6.1 %collective-permute-start.5 = (bf16[256,512]{1,0:T(8,128)(2,1)S(1)}, bf16[256,512]{1,0:T(8,128)(2,1)S(1)}, u32[]{:S(2)}, u32[]{:S(2)}) collective-permute-start(bf16[256,512]{1,0:T(8,128)(2,1)S(1)} %get-tuple-element.34), channel_id=1, source_target_pairs={{0,224},{32,64},{64,32},{96,128},{128,96},{160,192},{192,160},{224... | collective-permute-start | bytes 786440 | tf_op jit(solution)/shard_map/ppermute | solution.py:245
  27.7 18.4 %copy-start.1 = (f32[1024]{0:T(1024)S(1)}, f32[1024]{0:T(1024)}, u32[]{:S(2)}) copy-start(f32[1024]{0:T(1024)} %param.10) | copy-start | bytes 12292
  32.1 24.4 %copy-start.2 = (f32[1024]{0:T(1024)S(1)}, f32[1024]{0:T(1024)}, u32[]{:S(2)}) copy-start(f32[1024]{0:T(1024)} %param.11) | copy-start | bytes 12292

commit v6 on v5

--- a/solution.py
+++ b/solution.py
@@ -144,9 +144,12 @@
         x_far[:, across] = jnp.where(odd_s, last, first)
 
 
-def ends_kernel(left, r_far, src_ends, cost_tgt, hi, lo, small_tgt):
+def small_kernel(cost_tgt, small_tgt):
+    small_tgt[...] = (cost_tgt[...].astype(f32) * SCALE).astype(f8)
+
+
+def ends_kernel(left, r_far, src_ends, _, hi, lo):
     rows, cols = left.shape
-    small_tgt[...] = (cost_tgt[...].astype(f32) * SCALE).astype(f8)
     for across in tiles_of(cols):
         value = left[:, across] + dot(src_ends[:, H1:], r_far[:, across])
         hi[:, across], lo[:, across] = halves(value)
@@ -234,15 +237,22 @@
     )(*args)
 
 
-def pair_plans(size):
+def far_of(index, size):
+    return (index + 1 if index % 2 else index - 1) % size
+
+
+def exchange(first, second, axis):
+    n_src, n_tgt = lax.axis_size("src"), lax.axis_size("tgt")
+    size = lax.axis_size(axis)
     near = [(i, i ^ 1) for i in range(size)]
-    far = [(i, (i + 1 if i % 2 else i - 1) % size) for i in range(size)]
-    return near, far
-
-
-def exchange(first, second, axis):
-    near, far = pair_plans(lax.axis_size(axis))
-    return lax.ppermute(first, axis, near), lax.ppermute(second, axis, far)
+    far = []
+    for s in range(n_src):
+        for t in range(n_tgt):
+            to = (s, far_of(t, n_tgt)) if axis == "tgt" else (far_of(s, n_src), t)
+            if axis == "tgt" and t in (0, n_tgt - 1):
+                to = (s ^ 1, t)
+            far.append((s * n_tgt + t, to[0] * n_tgt + to[1]))
+    return lax.ppermute(first, axis, near), lax.ppermute(second, ("src", "tgt"), far)
 
 
 def per_device(coupling, cost_src, cost_tgt, pattern, mass_src, mass_tgt):
@@ -279,10 +289,11 @@
         moved=EST["left"],
     )
     m_near, m_far = exchange(m_near, m_far, "tgt")
-    hi, lo, small_tgt = call(
+    small_tgt = call(small_kernel, [cost_tgt], [(cost_tgt.shape, f8)], [], moved=MIB)
+    hi, lo = call(
         ends_kernel,
-        [left, r_far, src_ends, cost_tgt],
-        [((rows, cols), bf16), ((rows, cols), f8), (cost_tgt.shape, f8)],
+        [left, r_far, src_ends, small_tgt],
+        [((rows, cols), bf16), ((rows, cols), f8)],
         [],
         moved=EST["ends"],
     )

time: 58.9 us -> 58.4 us (level)
  starting transfers between devices: 16 us -> 10.9 us
  blocking collectives: 23.8 us -> 28.7 us
    ppermute x8, starting transfers between devices: 16 us -> 10.9 us  [the longest x4 5.8 us: exchange(): lax.ppermute(first, axis, near)]
    all_to_all x1, blocking collectives: 14 us -> 18.9 us  [per_device(): row_totals = lax.all_to_all(totals, 'tgt', 0, 0, tiled=True)]
    pallas_call x10 -> x11, Pallas kernels: 17.3 us -> 16.9 us  [call(): pl.pallas_call(body, out_shape=shapes[0] if single else shapes, in_specs=...]
  transfers between devices with their start and end apart: 8 -> 8, of which waited for: 1 -> 1; matrix products, arithmetic and copies ran while one was open for 0% -> 0% of each run, Pallas kernels for 17% -> 16%
where the time goes in v6:
time: 58.4 us; the launch traced here: 58.2 us
  blocking collectives  28.7 us (49%)
  Pallas kernels  16.9 us (29%)
  starting transfers between devices  10.9 us (19%)
  waiting for transfers between devices  1.35 us (2%)
    all_to_all x1, blocking collectives, per_device(): row_totals = lax.all_to_all(totals, 'tgt', 0, 0, tiled=True)  18.9 us
    pallas_call x11, Pallas kernels, call(): pl.pallas_call(body, out_shape=shapes[0] if single else shapes, in_specs=...  16.9 us
    all_to_all x1, blocking collectives, per_device(): col_totals = lax.all_to_all(totals, 'src', 0, 0, tiled=True)  9.81 us
    ppermute x4, starting transfers between devices, exchange(): lax.ppermute(first, axis, near)  5.8 us
    ppermute x4, starting transfers between devices, exchange(): lax.ppermute(second, ('src', 'tgt'), far)  5.12 us
    ppermute x4, waiting for transfers between devices, exchange(): lax.ppermute(second, ('src', 'tgt'), far)  1.34 us
  transfers between devices with their start and end apart: 8, of which 1 were waited for; matrix products, arithmetic and copies ran while one was open for 0% of the time, Pallas kernels for 16%

profile of v6, /device:TPU:1, one launch (start us, length us, event | category | flops | bytes accessed | tf_op | source)
XLA Modules:
  0.0 58.2 jit_solution(7207380003323625549)
XLA Ops:
  0.0 1.8 %shard_map.64 = (bf16[1024,1024]{1,0:T(8,128)(2,1)S(1)}, bf16[512,256]{1,0:T(8,128)(2,1)S(1)}, bf16[512,256]{1,0:T(8,128)(2,1)S(1)}) custom-call(s32[4,4]{1,0:T(4,128)} %pattern.1, bf16[1024,1024]{1,0:T(8,128)(2,1)} %coupling.1), custom_call_target="tpu_custom_call" | custom-call | bytes 6291456 | tf_op jit(solution)/shard_map/pallas_call | solution.py:229
  1.8 0.1 shard_map.65
  1.9 3.3 %collective-permute-start.2 = (bf16[256,1024]{1,0:T(8,128)(2,1)S(1)}, bf16[256,1024]{1,0:T(8,128)(2,1)S(1)}, u32[]{:S(2)}, u32[]{:S(2)}) collective-permute-start(bf16[256,1024]{1,0:T(8,128)(2,1)S(1)} %get-tuple-element.26), channel_id=1, source_target_pairs={{0,32},{32,0},{64,96},{96,64},{128,160},{160,128},{192,224},{224,1... | collective-permute-start | bytes 1572872 | tf_op jit(solution)/shard_map/ppermute | solution.py:255
  5.2 0.0 collective-permute-start.3
  5.2 1.2 %collective-permute-start = (bf16[512,256]{1,0:T(8,128)(2,1)S(1)}, bf16[512,256]{1,0:T(8,128)(2,1)S(1)}, u32[]{:S(2)}, u32[]{:S(2)}) collective-permute-start(bf16[512,256]{1,0:T(8,128)(2,1)S(1)} %get-tuple-element.23), channel_id=1, source_target_pairs={{0,1},{1,0},{2,3},{3,2},{4,5},{5,4},{6,7},{7,6},{8,9},{9,8},{10,11... | collective-permute-start | bytes 786440 | tf_op jit(solution)/shard_map/ppermute | solution.py:255
  6.4 2.1 %collective-permute-start.1 = (bf16[512,256]{1,0:T(8,128)(2,1)S(1)}, bf16[512,256]{1,0:T(8,128)(2,1)S(1)}, u32[]{:S(2)}, u32[]{:S(2)}) collective-permute-start(bf16[512,256]{1,0:T(8,128)(2,1)S(1)} %get-tuple-element.24), channel_id=1, source_target_pairs={{0,32},{1,2},{2,1},{3,4},{4,3},{5,6},{6,5},{7,8},{8,7},{9,10},{10,... | collective-permute-start | bytes 786440 | tf_op jit(solution)/shard_map/ppermute | solution.py:255
  8.5 3.1 %shard_map.66 = (bf16[512,256]{1,0:T(8,128)(2,1)S(1)}, bf16[512,256]{1,0:T(8,128)(2,1)S(1)}, f32[1024,1024]{1,0:T(8,128)S(1)}, bf16[1024,512]{1,0:T(8,128)(2,1)S(1)}, bf16[1024,1536]{1,0:T(8,128)(2,1)S(1)}) custom-call(bf16[1024,1024]{1,0:T(8,128)(2,1)S(1)} %get-tuple-element.25.masked, bf16[256,1024]{1,0:T(8,128)(2,1)S(1)} %collective-permute-done.2.r_near, ...), custom_call_target="tpu_custom_call" | custom-call | bytes 1048576 | tf_op jit(solution)/shard_map/pallas_call | solution.py:229
  11.6 1.2 %collective-permute-start.6 = (bf16[512,256]{1,0:T(8,128)(2,1)S(1)}, bf16[512,256]{1,0:T(8,128)(2,1)S(1)}, u32[]{:S(2)}, u32[]{:S(2)}) collective-permute-start(bf16[512,256]{1,0:T(8,128)(2,1)S(1)} %get-tuple-element.34), channel_id=1, source_target_pairs={{0,1},{1,0},{2,3},{3,2},{4,5},{5,4},{6,7},{7,6},{8,9},{9,8},{10,11... | collective-permute-start | bytes 786440 | tf_op jit(solution)/shard_map/ppermute | solution.py:255
  12.8 2.7 %collective-permute-start.7 = (bf16[512,256]{1,0:T(8,128)(2,1)S(1)}, bf16[512,256]{1,0:T(8,128)(2,1)S(1)}, u32[]{:S(2)}, u32[]{:S(2)}) collective-permute-start(bf16[512,256]{1,0:T(8,128)(2,1)S(1)} %get-tuple-element.35), channel_id=1, source_target_pairs={{0,32},{1,2},{2,1},{3,4},{4,3},{5,6},{6,5},{7,8},{8,7},{9,10},{10,... | collective-permute-start | bytes 786440 | tf_op jit(solution)/shard_map/ppermute | solution.py:255
  15.5 0.6 shard_map.67._.small_tgt
  16.1 1.0 %shard_map.68 = (bf16[1024,1024]{1,0:T(8,128)(2,1)S(1)}, f8e4m3fn[1024,1024]{1,0:T(32,128)(4,1)S(1)}) custom-call(f32[1024,1024]{1,0:T(8,128)S(1)} %get-tuple-element.27.left, bf16[256,1024]{1,0:T(8,128)(2,1)S(1)} %collective-permute-done.3.r_far, bf16[1024,512]{1,0:T(8,128)(2,1)S(1)} %get-tuple-element.29.src_ends, ...), custom_call_target="tpu_custom_call" | custom-call | bytes 1048576 | tf_op jit(solution)/shard_map/pallas_call | solution.py:229
  17.2 0.1 shard_map.69
  17.2 0.1 collective-permute-start.4
  17.3 0.3 collective-permute-start.5
  17.6 3.4 %shard_map.71.grad = f32[1024,1024]{1,0:T(8,128)S(1)} custom-call(bf16[1024,1024]{1,0:T(8,128)(2,1)S(1)} %get-tuple-element.36.hi, f8e4m3fn[1024,1024]{1,0:T(32,128)(4,1)S(1)} %get-tuple-element.31._.lo, bf16[1024,1536]{1,0:T(8,128)(2,1)S(1)} %get-tuple-element.30.cost_tgt, f8e4m3fn[1024,1536]{1,0:T(32,128)(4,1)S(1)} %shard_map.67._.small_tgt), custom_call_target="tpu_custom_call" | custom-call | bytes 1048576 | tf_op jit(solution)/shard_map/pallas_call | solution.py:229
  21.1 1.2 %shard_map.70.sides = f32[1024,512]{1,0:T(8,128)S(1)} custom-call(bf16[512,256]{1,0:T(8,128)(2,1)S(1)} %collective-permute-done.e_near, bf16[512,256]{1,0:T(8,128)(2,1)S(1)} %collective-permute-done.1.e_far, bf16[512,256]{1,0:T(8,128)(2,1)S(1)} %collective-permute-done.6.m_near, bf16[512,256]{1,0:T(8,128)(2,1)S(1)} %collective-permute-done.7.m_far, ...), custom_call_target="tpu_custom_call" | custom-call | bytes 1048576 | tf_op jit(solution)/shard_map/pallas_call | solution.py:229
  22.3 0.0 copy-start.1
  22.3 1.3 %collective-permute-done.5.x_far = bf16[256,512]{1,0:T(8,128)(2,1)S(1)} collective-permute-done((bf16[256,512]{1,0:T(8,128)(2,1)S(1)}, bf16[256,512]{1,0:T(8,128)(2,1)S(1)}, u32[]{:S(2)}, u32[]{:S(2)}) %collective-permute-start.5) | collective-permute-done | bytes 262176 | tf_op jit(solution)/shard_map/ppermute | solution.py:255
  23.7 2.9 %shard_map.72 = (f32[1024,1024]{1,0:T(8,128)S(1)}, f32[32,1,1024]{2,1,0:T(1,128)S(1)}) custom-call(bf16[256,512]{1,0:T(8,128)(2,1)S(1)} %collective-permute-done.4.x_near, bf16[256,512]{1,0:T(8,128)(2,1)S(1)} %collective-permute-done.5.x_far, f32[1024,512]{1,0:T(8,128)S(1)} %shard_map.70.sides, bf16[1024,512]{1,0:T(8,128)(2,1)S(1)} %get-tuple-element.29.src_ends, ...), custom_call_target="tpu_custom_call" | custom-call | bytes 1048576 | tf_op jit(solution)/shard_map/pallas_call | solution.py:229
  26.6 0.0 copy-start.2
  26.6 18.9 %all_to_all.10.refs_0_ = f32[32,1,1024]{2,1,0:T(1,128)S(1)} all-to-all(f32[32,1,1024]{2,1,0:T(1,128)S(1)} %get-tuple-element.37), channel_id=1, replica_groups=mesh['src'=8,'tgt'=32] {'tgt'}, dimensions={0} | all-to-all | bytes 262144 | tf_op jit(solution)/shard_map/all_to_all | solution.py:325
  45.6 0.5 shard_map.73
  46.1 9.8 %all_to_all.11.refs_0_ = f32[8,1,1024]{2,1,0:T(1,128)S(1)} all-to-all(f32[8,1,1024]{2,1,0:T(1,128)S(1)} %get-tuple-element.39), channel_id=1, replica_groups=mesh['src'=8,'tgt'=32] {'src'}, dimensions={0} | all-to-all | bytes 65536 | tf_op jit(solution)/shard_map/all_to_all | solution.py:333
  55.9 2.1 %shard_map.74 = f32[1024,1024]{1,0:T(8,128)} custom-call(f32[8,1,1024]{2,1,0:T(1,128)S(1)} %all_to_all.11.refs_0_, f32[1,1024]{1,0:T(1,128)S(1)} %bitcast.3, f32[1024,1024]{1,0:T(8,128)S(1)} %get-tuple-element.40.refs_2_), custom_call_target="tpu_custom_call" | custom-call | bytes 8388608 | tf_op jit(solution)/shard_map/pallas_call | solution.py:229
  (11 shorter events, 0.0 us)
Async XLA Ops:
  0.0 8.5 %copy-start = (bf16[1024,1536]{1,0:T(8,128)(2,1)S(1)}, bf16[1024,1536]{1,0:T(8,128)(2,1)}, u32[]{:S(2)}) copy-start(bf16[1024,1536]{1,0:T(8,128)(2,1)} %cost_src.3) | copy-start | bytes 9437188
  1.9 6.6 %collective-permute-start.2 = (bf16[256,1024]{1,0:T(8,128)(2,1)S(1)}, bf16[256,1024]{1,0:T(8,128)(2,1)S(1)}, u32[]{:S(2)}, u32[]{:S(2)}) collective-permute-start(bf16[256,1024]{1,0:T(8,128)(2,1)S(1)} %get-tuple-element.26), channel_id=1, source_target_pairs={{0,32},{32,0},{64,96},{96,64},{128,160},{160,128},{192,224},{224,1... | collective-permute-start | bytes 1572872 | tf_op jit(solution)/shard_map/ppermute | solution.py:255
  5.2 10.9 %collective-permute-start.3 = (bf16[256,1024]{1,0:T(8,128)(2,1)S(1)}, bf16[256,1024]{1,0:T(8,128)(2,1)S(1)}, u32[]{:S(2)}, u32[]{:S(2)}) collective-permute-start(bf16[256,1024]{1,0:T(8,128)(2,1)S(1)} %get-tuple-element.28), channel_id=1, source_target_pairs={{0,224},{1,225},{2,226},{3,227},{4,228},{5,229},{6,230},{7,231},{8... | collective-permute-start | bytes 1572872 | tf_op jit(solution)/shard_map/ppermute | solution.py:255
  5.2 11.9 %collective-permute-start = (bf16[512,256]{1,0:T(8,128)(2,1)S(1)}, bf16[512,256]{1,0:T(8,128)(2,1)S(1)}, u32[]{:S(2)}, u32[]{:S(2)}) collective-permute-start(bf16[512,256]{1,0:T(8,128)(2,1)S(1)} %get-tuple-element.23), channel_id=1, source_target_pairs={{0,1},{1,0},{2,3},{3,2},{4,5},{5,4},{6,7},{7,6},{8,9},{9,8},{10,11... | collective-permute-start | bytes 786440 | tf_op jit(solution)/shard_map/ppermute | solution.py:255
  6.4 10.7 %collective-permute-start.1 = (bf16[512,256]{1,0:T(8,128)(2,1)S(1)}, bf16[512,256]{1,0:T(8,128)(2,1)S(1)}, u32[]{:S(2)}, u32[]{:S(2)}) collective-permute-start(bf16[512,256]{1,0:T(8,128)(2,1)S(1)} %get-tuple-element.24), channel_id=1, source_target_pairs={{0,32},{1,2},{2,1},{3,4},{4,3},{5,6},{6,5},{7,8},{8,7},{9,10},{10,... | collective-permute-start | bytes 786440 | tf_op jit(solution)/shard_map/ppermute | solution.py:255
  11.6 9.4 %collective-permute-start.6 = (bf16[512,256]{1,0:T(8,128)(2,1)S(1)}, bf16[512,256]{1,0:T(8,128)(2,1)S(1)}, u32[]{:S(2)}, u32[]{:S(2)}) collective-permute-start(bf16[512,256]{1,0:T(8,128)(2,1)S(1)} %get-tuple-element.34), channel_id=1, source_target_pairs={{0,1},{1,0},{2,3},{3,2},{4,5},{5,4},{6,7},{7,6},{8,9},{9,8},{10,11... | collective-permute-start | bytes 786440 | tf_op jit(solution)/shard_map/ppermute | solution.py:255
  12.8 8.2 %collective-permute-start.7 = (bf16[512,256]{1,0:T(8,128)(2,1)S(1)}, bf16[512,256]{1,0:T(8,128)(2,1)S(1)}, u32[]{:S(2)}, u32[]{:S(2)}) collective-permute-start(bf16[512,256]{1,0:T(8,128)(2,1)S(1)} %get-tuple-element.35), channel_id=1, source_target_pairs={{0,32},{1,2},{2,1},{3,4},{4,3},{5,6},{6,5},{7,8},{8,7},{9,10},{10,... | collective-permute-start | bytes 786440 | tf_op jit(solution)/shard_map/ppermute | solution.py:255
  17.2 5.1 %collective-permute-start.4 = (bf16[256,512]{1,0:T(8,128)(2,1)S(1)}, bf16[256,512]{1,0:T(8,128)(2,1)S(1)}, u32[]{:S(2)}, u32[]{:S(2)}) collective-permute-start(bf16[256,512]{1,0:T(8,128)(2,1)S(1)} %get-tuple-element.32), channel_id=1, source_target_pairs={{0,32},{32,0},{64,96},{96,64},{128,160},{160,128},{192,224},{224,1... | collective-permute-start | bytes 786440 | tf_op jit(solution)/shard_map/ppermute | solution.py:255
  17.3 6.4 %collective-permute-start.5 = (bf16[256,512]{1,0:T(8,128)(2,1)S(1)}, bf16[256,512]{1,0:T(8,128)(2,1)S(1)}, u32[]{:S(2)}, u32[]{:S(2)}) collective-permute-start(bf16[256,512]{1,0:T(8,128)(2,1)S(1)} %get-tuple-element.33), channel_id=1, source_target_pairs={{0,224},{1,225},{2,226},{3,227},{4,228},{5,229},{6,230},{7,231},{8... | collective-permute-start | bytes 786440 | tf_op jit(solution)/shard_map/ppermute | solution.py:255
  22.3 23.2 %copy-start.1 = (f32[1024]{0:T(1024)S(1)}, f32[1024]{0:T(1024)}, u32[]{:S(2)}) copy-start(f32[1024]{0:T(1024)} %param.10) | copy-start | bytes 12292
  26.6 29.3 %copy-start.2 = (f32[1024]{0:T(1024)S(1)}, f32[1024]{0:T(1024)}, u32[]{:S(2)}) copy-start(f32[1024]{0:T(1024)} %param.11) | copy-start | bytes 12292

commit v7 on v6

--- a/solution.py
+++ b/solution.py
@@ -187,20 +187,19 @@
     totals[...] = jnp.broadcast_to(as_row(part[...])[None], totals.shape)
 
 
-def column_kernel(total, row_totals, mass, kernel, scaled, totals):
+def column_kernel(total, row_totals, mass, kernel, rows_by, totals):
     rows, cols = kernel.shape
     factor = mass[...] * total / jnp.sum(row_totals[...], axis=0)
     factor = jnp.broadcast_to(factor, (LANES, rows)).T
+    rows_by[...] = factor
     for n in range(cols // LANES):
         across = slice(n * LANES, (n + 1) * LANES)
-        value = kernel[:, across] * factor
-        scaled[:, across] = value
-        sums = jnp.sum(value, axis=0, keepdims=True)
+        sums = jnp.sum(kernel[:, across] * factor, axis=0, keepdims=True)
         totals[:, :, across] = jnp.broadcast_to(sums[None], (totals.shape[0], 1, LANES))
 
 
-def last_kernel(total, col_totals, mass, scaled, out, block, sems):
-    rows, cols = scaled.shape
+def last_kernel(total, col_totals, mass, rows_by, kernel, out, block, sems):
+    rows, cols = kernel.shape
     factor = mass[...] * total / jnp.sum(col_totals[...], axis=0)
     n_blocks = sems.shape[0]
     size = rows // n_blocks
@@ -211,7 +210,9 @@
 
     for n in range(n_blocks):
         part = slice(n * size, (n + 1) * size)
-        block[part, :] = scaled[part, :] * factor
+        for k in range(cols // LANES):
+            across = slice(k * LANES, (k + 1) * LANES)
+            block[part, across] = kernel[part, across] * rows_by[part, :] * factor[:, across]
         copy(n).start()
     for n in range(n_blocks):
         copy(n).wait()
@@ -323,17 +324,17 @@
         moved=EST["tail"],
     )
     row_totals = lax.all_to_all(totals, "tgt", 0, 0, tiled=True)
-    scaled, totals = call(
+    rows_by, totals = call(
         lambda *refs: column_kernel(float(cols * n_tgt), *refs),
         [row_totals, mass_src[None, :], kernel],
-        [((rows, cols), f32), ((n_src, 1, cols), f32)],
+        [((rows, LANES), f32), ((n_src, 1, cols), f32)],
         [],
         moved=8 * MIB,
     )
     col_totals = lax.all_to_all(totals, "src", 0, 0, tiled=True)
     return call(
         lambda *refs: last_kernel(float(rows * n_src), *refs),
-        [col_totals, mass_tgt[None, :], scaled],
+        [col_totals, mass_tgt[None, :], rows_by, kernel],
         [jax.ShapeDtypeStruct((rows, cols), f32)],
         [VMEM((rows, cols), f32), dma((8,))],
         moved=8 * MIB,

time: 58.4 us -> 58.4 us (level)
  no operation moved by 1% of the time
where the time goes in v7:
time: 58.4 us; the launch traced here: 58.2 us
  blocking collectives  28.7 us (49%)
  Pallas kernels  16.8 us (29%)
  starting transfers between devices  10.9 us (19%)
  waiting for transfers between devices  1.36 us (2%)
    all_to_all x1, blocking collectives, per_device(): row_totals = lax.all_to_all(totals, 'tgt', 0, 0, tiled=True)  18.9 us
    pallas_call x11, Pallas kernels, call(): pl.pallas_call(body, out_shape=shapes[0] if single else shapes, in_specs=...  16.8 us
    all_to_all x1, blocking collectives, per_device(): col_totals = lax.all_to_all(totals, 'src', 0, 0, tiled=True)  9.81 us
    ppermute x4, starting transfers between devices, exchange(): lax.ppermute(first, axis, near)  5.8 us
    ppermute x4, starting transfers between devices, exchange(): lax.ppermute(second, ('src', 'tgt'), far)  5.13 us
    ppermute x4, waiting for transfers between devices, exchange(): lax.ppermute(second, ('src', 'tgt'), far)  1.35 us
  transfers between devices with their start and end apart: 8, of which 1 were waited for; matrix products, arithmetic and copies ran while one was open for 0% of the time, Pallas kernels for 16%

profile of v7, /device:TPU:1, one launch (start us, length us, event | category | flops | bytes accessed | tf_op | source)
XLA Modules:
  0.0 58.2 jit_solution(10666405371079366030)
XLA Ops:
  0.0 1.8 %shard_map.64 = (bf16[1024,1024]{1,0:T(8,128)(2,1)S(1)}, bf16[512,256]{1,0:T(8,128)(2,1)S(1)}, bf16[512,256]{1,0:T(8,128)(2,1)S(1)}) custom-call(s32[4,4]{1,0:T(4,128)} %pattern.1, bf16[1024,1024]{1,0:T(8,128)(2,1)} %coupling.1), custom_call_target="tpu_custom_call" | custom-call | bytes 6291456 | tf_op jit(solution)/shard_map/pallas_call | solution.py:230
  1.8 0.1 shard_map.65
  1.9 3.3 %collective-permute-start.2 = (bf16[256,1024]{1,0:T(8,128)(2,1)S(1)}, bf16[256,1024]{1,0:T(8,128)(2,1)S(1)}, u32[]{:S(2)}, u32[]{:S(2)}) collective-permute-start(bf16[256,1024]{1,0:T(8,128)(2,1)S(1)} %get-tuple-element.26), channel_id=1, source_target_pairs={{0,32},{32,0},{64,96},{96,64},{128,160},{160,128},{192,224},{224,1... | collective-permute-start | bytes 1572872 | tf_op jit(solution)/shard_map/ppermute | solution.py:256
  5.2 1.2 %collective-permute-start = (bf16[512,256]{1,0:T(8,128)(2,1)S(1)}, bf16[512,256]{1,0:T(8,128)(2,1)S(1)}, u32[]{:S(2)}, u32[]{:S(2)}) collective-permute-start(bf16[512,256]{1,0:T(8,128)(2,1)S(1)} %get-tuple-element.23), channel_id=1, source_target_pairs={{0,1},{1,0},{2,3},{3,2},{4,5},{5,4},{6,7},{7,6},{8,9},{9,8},{10,11... | collective-permute-start | bytes 786440 | tf_op jit(solution)/shard_map/ppermute | solution.py:256
  6.4 2.1 %collective-permute-start.1 = (bf16[512,256]{1,0:T(8,128)(2,1)S(1)}, bf16[512,256]{1,0:T(8,128)(2,1)S(1)}, u32[]{:S(2)}, u32[]{:S(2)}) collective-permute-start(bf16[512,256]{1,0:T(8,128)(2,1)S(1)} %get-tuple-element.24), channel_id=1, source_target_pairs={{0,32},{1,2},{2,1},{3,4},{4,3},{5,6},{6,5},{7,8},{8,7},{9,10},{10,... | collective-permute-start | bytes 786440 | tf_op jit(solution)/shard_map/ppermute | solution.py:256
  8.5 0.0 collective-permute-done.2.r_near
  8.5 3.1 %shard_map.66 = (bf16[512,256]{1,0:T(8,128)(2,1)S(1)}, bf16[512,256]{1,0:T(8,128)(2,1)S(1)}, f32[1024,1024]{1,0:T(8,128)S(1)}, bf16[1024,512]{1,0:T(8,128)(2,1)S(1)}, bf16[1024,1536]{1,0:T(8,128)(2,1)S(1)}) custom-call(bf16[1024,1024]{1,0:T(8,128)(2,1)S(1)} %get-tuple-element.25.masked, bf16[256,1024]{1,0:T(8,128)(2,1)S(1)} %collective-permute-done.2.r_near, ...), custom_call_target="tpu_custom_call" | custom-call | bytes 1048576 | tf_op jit(solution)/shard_map/pallas_call | solution.py:230
  11.6 1.2 %collective-permute-start.6 = (bf16[512,256]{1,0:T(8,128)(2,1)S(1)}, bf16[512,256]{1,0:T(8,128)(2,1)S(1)}, u32[]{:S(2)}, u32[]{:S(2)}) collective-permute-start(bf16[512,256]{1,0:T(8,128)(2,1)S(1)} %get-tuple-element.34), channel_id=1, source_target_pairs={{0,1},{1,0},{2,3},{3,2},{4,5},{5,4},{6,7},{7,6},{8,9},{9,8},{10,11... | collective-permute-start | bytes 786440 | tf_op jit(solution)/shard_map/ppermute | solution.py:256
  12.8 2.7 %collective-permute-start.7 = (bf16[512,256]{1,0:T(8,128)(2,1)S(1)}, bf16[512,256]{1,0:T(8,128)(2,1)S(1)}, u32[]{:S(2)}, u32[]{:S(2)}) collective-permute-start(bf16[512,256]{1,0:T(8,128)(2,1)S(1)} %get-tuple-element.35), channel_id=1, source_target_pairs={{0,32},{1,2},{2,1},{3,4},{4,3},{5,6},{6,5},{7,8},{8,7},{9,10},{10,... | collective-permute-start | bytes 786440 | tf_op jit(solution)/shard_map/ppermute | solution.py:256
  15.5 0.6 shard_map.67._.small_tgt
  16.1 1.0 %shard_map.68 = (bf16[1024,1024]{1,0:T(8,128)(2,1)S(1)}, f8e4m3fn[1024,1024]{1,0:T(32,128)(4,1)S(1)}) custom-call(f32[1024,1024]{1,0:T(8,128)S(1)} %get-tuple-element.27.left, bf16[256,1024]{1,0:T(8,128)(2,1)S(1)} %collective-permute-done.3.r_far, bf16[1024,512]{1,0:T(8,128)(2,1)S(1)} %get-tuple-element.29.src_ends, ...), custom_call_target="tpu_custom_call" | custom-call | bytes 1048576 | tf_op jit(solution)/shard_map/pallas_call | solution.py:230
  17.2 0.1 shard_map.69
  17.2 0.1 collective-permute-start.4
  17.3 0.3 collective-permute-start.5
  17.6 3.4 %shard_map.71.grad = f32[1024,1024]{1,0:T(8,128)S(1)} custom-call(bf16[1024,1024]{1,0:T(8,128)(2,1)S(1)} %get-tuple-element.36.hi, f8e4m3fn[1024,1024]{1,0:T(32,128)(4,1)S(1)} %get-tuple-element.31._.lo, bf16[1024,1536]{1,0:T(8,128)(2,1)S(1)} %get-tuple-element.30.cost_tgt, f8e4m3fn[1024,1536]{1,0:T(32,128)(4,1)S(1)} %shard_map.67._.small_tgt), custom_call_target="tpu_custom_call" | custom-call | bytes 1048576 | tf_op jit(solution)/shard_map/pallas_call | solution.py:230
  21.1 1.2 %shard_map.70.sides = f32[1024,512]{1,0:T(8,128)S(1)} custom-call(bf16[512,256]{1,0:T(8,128)(2,1)S(1)} %collective-permute-done.e_near, bf16[512,256]{1,0:T(8,128)(2,1)S(1)} %collective-permute-done.1.e_far, bf16[512,256]{1,0:T(8,128)(2,1)S(1)} %collective-permute-done.6.m_near, bf16[512,256]{1,0:T(8,128)(2,1)S(1)} %collective-permute-done.7.m_far, ...), custom_call_target="tpu_custom_call" | custom-call | bytes 1048576 | tf_op jit(solution)/shard_map/pallas_call | solution.py:230
  22.3 0.0 copy-start.1
  22.3 1.3 %collective-permute-done.5.x_far = bf16[256,512]{1,0:T(8,128)(2,1)S(1)} collective-permute-done((bf16[256,512]{1,0:T(8,128)(2,1)S(1)}, bf16[256,512]{1,0:T(8,128)(2,1)S(1)}, u32[]{:S(2)}, u32[]{:S(2)}) %collective-permute-start.5) | collective-permute-done | bytes 262176 | tf_op jit(solution)/shard_map/ppermute | solution.py:256
  23.7 2.9 %shard_map.72 = (f32[1024,1024]{1,0:T(8,128)S(1)}, f32[32,1,1024]{2,1,0:T(1,128)S(1)}) custom-call(bf16[256,512]{1,0:T(8,128)(2,1)S(1)} %collective-permute-done.4.x_near, bf16[256,512]{1,0:T(8,128)(2,1)S(1)} %collective-permute-done.5.x_far, f32[1024,512]{1,0:T(8,128)S(1)} %shard_map.70.sides, bf16[1024,512]{1,0:T(8,128)(2,1)S(1)} %get-tuple-element.29.src_ends, ...), custom_call_target="tpu_custom_call" | custom-call | bytes 1048576 | tf_op jit(solution)/shard_map/pallas_call | solution.py:230
  26.6 0.0 copy-start.2
  26.6 18.9 %all_to_all.10.refs_0_ = f32[32,1,1024]{2,1,0:T(1,128)S(1)} all-to-all(f32[32,1,1024]{2,1,0:T(1,128)S(1)} %get-tuple-element.37), channel_id=1, replica_groups=mesh['src'=8,'tgt'=32] {'tgt'}, dimensions={0} | all-to-all | bytes 262144 | tf_op jit(solution)/shard_map/all_to_all | solution.py:326
  45.6 0.5 shard_map.73
  46.1 9.8 %all_to_all.11.refs_0_ = f32[8,1,1024]{2,1,0:T(1,128)S(1)} all-to-all(f32[8,1,1024]{2,1,0:T(1,128)S(1)} %get-tuple-element.39), channel_id=1, replica_groups=mesh['src'=8,'tgt'=32] {'src'}, dimensions={0} | all-to-all | bytes 65536 | tf_op jit(solution)/shard_map/all_to_all | solution.py:334
  55.9 2.2 %shard_map.74 = f32[1024,1024]{1,0:T(8,128)} custom-call(f32[8,1,1024]{2,1,0:T(1,128)S(1)} %all_to_all.11.refs_0_, f32[1,1024]{1,0:T(1,128)S(1)} %bitcast.3, f32[1024,128]{1,0:T(8,128)S(1)} %get-tuple-element.40.refs_2_, f32[1024,1024]{1,0:T(8,128)S(1)} %get-tuple-element.38.refs_2_.refs_3_), custom_call_target="tpu_custom_call" | custom-call | bytes 8388608 | tf_op jit(solution)/shard_map/pallas_call | solution.py:230
  (11 shorter events, 0.0 us)
Async XLA Ops:
  0.0 8.5 %copy-start = (bf16[1024,1536]{1,0:T(8,128)(2,1)S(1)}, bf16[1024,1536]{1,0:T(8,128)(2,1)}, u32[]{:S(2)}) copy-start(bf16[1024,1536]{1,0:T(8,128)(2,1)} %cost_src.3) | copy-start | bytes 9437188
  1.9 6.6 %collective-permute-start.2 = (bf16[256,1024]{1,0:T(8,128)(2,1)S(1)}, bf16[256,1024]{1,0:T(8,128)(2,1)S(1)}, u32[]{:S(2)}, u32[]{:S(2)}) collective-permute-start(bf16[256,1024]{1,0:T(8,128)(2,1)S(1)} %get-tuple-element.26), channel_id=1, source_target_pairs={{0,32},{32,0},{64,96},{96,64},{128,160},{160,128},{192,224},{224,1... | collective-permute-start | bytes 1572872 | tf_op jit(solution)/shard_map/ppermute | solution.py:256
  5.2 10.9 %collective-permute-start.3 = (bf16[256,1024]{1,0:T(8,128)(2,1)S(1)}, bf16[256,1024]{1,0:T(8,128)(2,1)S(1)}, u32[]{:S(2)}, u32[]{:S(2)}) collective-permute-start(bf16[256,1024]{1,0:T(8,128)(2,1)S(1)} %get-tuple-element.28), channel_id=1, source_target_pairs={{0,224},{1,225},{2,226},{3,227},{4,228},{5,229},{6,230},{7,231},{8... | collective-permute-start | bytes 1572872 | tf_op jit(solution)/shard_map/ppermute | solution.py:256
  5.2 11.9 %collective-permute-start = (bf16[512,256]{1,0:T(8,128)(2,1)S(1)}, bf16[512,256]{1,0:T(8,128)(2,1)S(1)}, u32[]{:S(2)}, u32[]{:S(2)}) collective-permute-start(bf16[512,256]{1,0:T(8,128)(2,1)S(1)} %get-tuple-element.23), channel_id=1, source_target_pairs={{0,1},{1,0},{2,3},{3,2},{4,5},{5,4},{6,7},{7,6},{8,9},{9,8},{10,11... | collective-permute-start | bytes 786440 | tf_op jit(solution)/shard_map/ppermute | solution.py:256
  6.4 10.7 %collective-permute-start.1 = (bf16[512,256]{1,0:T(8,128)(2,1)S(1)}, bf16[512,256]{1,0:T(8,128)(2,1)S(1)}, u32[]{:S(2)}, u32[]{:S(2)}) collective-permute-start(bf16[512,256]{1,0:T(8,128)(2,1)S(1)} %get-tuple-element.24), channel_id=1, source_target_pairs={{0,32},{1,2},{2,1},{3,4},{4,3},{5,6},{6,5},{7,8},{8,7},{9,10},{10,... | collective-permute-start | bytes 786440 | tf_op jit(solution)/shard_map/ppermute | solution.py:256
  11.6 9.4 %collective-permute-start.6 = (bf16[512,256]{1,0:T(8,128)(2,1)S(1)}, bf16[512,256]{1,0:T(8,128)(2,1)S(1)}, u32[]{:S(2)}, u32[]{:S(2)}) collective-permute-start(bf16[512,256]{1,0:T(8,128)(2,1)S(1)} %get-tuple-element.34), channel_id=1, source_target_pairs={{0,1},{1,0},{2,3},{3,2},{4,5},{5,4},{6,7},{7,6},{8,9},{9,8},{10,11... | collective-permute-start | bytes 786440 | tf_op jit(solution)/shard_map/ppermute | solution.py:256
  12.8 8.2 %collective-permute-start.7 = (bf16[512,256]{1,0:T(8,128)(2,1)S(1)}, bf16[512,256]{1,0:T(8,128)(2,1)S(1)}, u32[]{:S(2)}, u32[]{:S(2)}) collective-permute-start(bf16[512,256]{1,0:T(8,128)(2,1)S(1)} %get-tuple-element.35), channel_id=1, source_target_pairs={{0,32},{1,2},{2,1},{3,4},{4,3},{5,6},{6,5},{7,8},{8,7},{9,10},{10,... | collective-permute-start | bytes 786440 | tf_op jit(solution)/shard_map/ppermute | solution.py:256
  17.2 5.1 %collective-permute-start.4 = (bf16[256,512]{1,0:T(8,128)(2,1)S(1)}, bf16[256,512]{1,0:T(8,128)(2,1)S(1)}, u32[]{:S(2)}, u32[]{:S(2)}) collective-permute-start(bf16[256,512]{1,0:T(8,128)(2,1)S(1)} %get-tuple-element.32), channel_id=1, source_target_pairs={{0,32},{32,0},{64,96},{96,64},{128,160},{160,128},{192,224},{224,1... | collective-permute-start | bytes 786440 | tf_op jit(solution)/shard_map/ppermute | solution.py:256
  17.3 6.4 %collective-permute-start.5 = (bf16[256,512]{1,0:T(8,128)(2,1)S(1)}, bf16[256,512]{1,0:T(8,128)(2,1)S(1)}, u32[]{:S(2)}, u32[]{:S(2)}) collective-permute-start(bf16[256,512]{1,0:T(8,128)(2,1)S(1)} %get-tuple-element.33), channel_id=1, source_target_pairs={{0,224},{1,225},{2,226},{3,227},{4,228},{5,229},{6,230},{7,231},{8... | collective-permute-start | bytes 786440 | tf_op jit(solution)/shard_map/ppermute | solution.py:256
  22.3 23.2 %copy-start.1 = (f32[1024]{0:T(1024)S(1)}, f32[1024]{0:T(1024)}, u32[]{:S(2)}) copy-start(f32[1024]{0:T(1024)} %param.10) | copy-start | bytes 12292
  26.6 29.2 %copy-start.2 = (f32[1024]{0:T(1024)S(1)}, f32[1024]{0:T(1024)}, u32[]{:S(2)}) copy-start(f32[1024]{0:T(1024)} %param.11) | copy-start | bytes 12292
